TPU v7x, 128 devices: a whole 4x4x4 slice. The times are simulated.
128 devices in a mesh: rows: 32 (over x, y, core), cols: 4 (over z).
Axes of the slice: x: 4, y: 4, z: 4, core: 2. Of those that a mesh axis runs over, the one named last changes fastest.
Arguments:
- latent_tokens: bfloat16 [8, 6656, 64], P(None, 'rows'), may hold values from -6 to 6
- cache_latent: bfloat16 [8, 2, 320, 112, 16], P(None, None, 'rows', 'cols'), may hold values from -6 to 6
- cache_middle: bfloat16 [8, 2, 320, 112, 384], P(None, None, 'rows', 'cols'), may hold values from -6 to 6
- entry_weight: bfloat16 [3, 3, 3, 16, 384], replicated, may hold values from -0.3125 to 0.3125
- time_weight: bfloat16 [3, 384, 768], replicated, may hold values from -0.1875 to 0.1875
- up_weight: bfloat16 [3, 3, 384, 192], replicated, may hold values from -0.109375 to 0.109375
- norm_gain: float32 [192], replicated, may hold values from 0.5 to 1.5
- row_ramp: int32 [32], replicated, may hold values from 2 to 4, as said below
- col_ramp: int32 [4], replicated, may hold values from 2 to 4, as said below
Outputs:
- blended: bfloat16 [8, 512, 208, 384], P(None, 'rows', 'cols')
Inputs may be any that keep to these rules, and one draw needn't show every extreme that they name: `row_ramp`: entry t, t >= 1, is the ramp length in output cells at the boundary between tiles t - 1 and t; entry 0 is not read. `col_ramp`: entry t, t >= 1, is the ramp length in output cells at the boundary between tiles t - 1 and t; entry 0 is not read.
All inputs are finite; a program needn't handle non-finite values.
Results may differ from a plain program's by a relative error of at most 0.0054.
Values may be sent and summed in bfloat16 or wider, within the bound.
No kernel may reach another device: no remote copies, remote signals or barrier semaphores. Data moves between devices by JAX's collectives and lax.ppermute only.
A program may use at most 192 MiB of HBM per device.

v0:
```python
import functools

import jax
import jax.numpy as jnp
from jax import lax
from jax.experimental import pallas as pl
from jax.experimental.pallas import tpu as pltpu
from jax.sharding import PartitionSpec as P

EPSILON = 1e-06
BF = jnp.bfloat16
F32 = jnp.float32
VID, C, U = 8, 384, 192
TR, TC = 10, 28
ROWS, COLS = 32, 4
NT = (((1,), (1,)), ((), ()))


def shift(value, axis, step):
    size = lax.axis_size(axis)
    pairs = [(i, i + step) for i in range(size) if 0 <= i + step < size]
    return lax.ppermute(value, axis, pairs)


VM = pl.BlockSpec(memory_space=pltpu.VMEM)
LIMIT = pltpu.CompilerParams(vmem_limit_bytes=24 << 20)


def held(value):
    return pltpu.with_memory_space_constraint(value, pltpu.VMEM)


def call(body, name, outs, args, flops, scratch=(), out_specs=None, smem=0):
    specs = [pl.BlockSpec(memory_space=pltpu.SMEM)] * smem + [VM] * (len(args) - smem)
    args = list(args[:smem]) + [held(v) for v in args[smem:]]
    return pl.pallas_call(
        body,
        in_specs=specs,
        out_specs=jax.tree.map(lambda _: VM, outs) if out_specs is None else out_specs,
        out_shape=outs,
        scratch_shapes=list(scratch),
        compiler_params=LIMIT,
        cost_estimate=pl.CostEstimate(flops=flops, bytes_accessed=1 << 16, transcendentals=0),
        name=name,
    )(*args)


WIDE = (TC + 2) * VID
PITCH = 56
STEPS = 5


def gather_body(col, tok_ref, before_ref, after_ref, cache_ref, x_ref, t_ref, lat_ref, old_ref):
    lat_ref[...] = jnp.zeros(lat_ref.shape, F32)
    old_ref[...] = jnp.zeros(old_ref.shape, F32)
    t_ref[...] = jnp.zeros(t_ref.shape, F32)
    for v in range(VID):
        own = jnp.transpose(tok_ref[v].astype(F32))
        rows = [jnp.transpose(before_ref[v].astype(F32))]
        rows += [own[52 * i : 52 * (i + 1)] for i in range(4)]
        rows += [jnp.transpose(after_ref[v].astype(F32))]
        for i in range(6):
            t_ref[v % 2, pl.ds(i * PITCH + 1, 52), 0:64] = rows[i]
        for i in range(6):
            near = t_ref[v % 2, pl.ds(i * PITCH + 13 * col, 15), :]
            for q in range(2):
                e = 2 * i + q
                if e in (0, 11):
                    continue
                for k in range(2):
                    part = pltpu.roll(near, (32 - (2 * q + k) * 16) % 128, 1)
                    part = part[1:15] if k == 0 else part[0:14]
                    first = 2 if k == 0 else 1
                    lat_ref[pl.ds((e * (TC + 2) + first) * VID + v, 14, stride=2 * VID), :] = part
        for t in range(TR):
            both = jnp.concatenate([cache_ref[v, 0, t], cache_ref[v, 1, t]], axis=0).astype(F32)
            both = jnp.concatenate([both, jnp.zeros((96, TC), F32)], axis=0)
            old_ref[pl.ds(((t + 1) * (TC + 2) + 1) * VID + v, TC, stride=VID), :] = jnp.transpose(both)
    lane = lax.broadcasted_iota(jnp.int32, (1, 128), 1)
    x_ref[...] = jnp.where(lane < 32, old_ref[...], jnp.where(lane < 48, lat_ref[...], 0.0)).astype(BF)


def mix_body(
    pos_ref,
    tok_ref,
    before_ref,
    after_ref,
    cache_ref,
    ew_ref,
    cm_hbm,
    wt_hbm,
    d_ref,
    x_ref,
    t_ref,
    lat_ref,
    old_ref,
    we_ref,
    cm_ref,
    wt_ref,
    sem,
):
    rows = TR // STEPS
    m = rows * TC * VID
    loads = [
        pltpu.make_async_copy(cm_hbm.at[pl.ds(g * m, m)], cm_ref.at[pl.ds(g * m, m)], sem.at[g]) for g in range(STEPS)
    ]
    load_wt = pltpu.make_async_copy(wt_hbm, wt_ref, sem.at[STEPS])
    loads[0].start()
    load_wt.start()
    for load in loads[1:]:
        load.start()
    edge = jnp.zeros((TR + 2, 1, 2 * VID, C), BF)
    d_ref[:, 0:1] = edge
    d_ref[:, TC + 1 : TC + 2] = edge
    line = jnp.zeros((1, TC + 2, 2 * VID, C), BF)
    d_ref[0:1] = line
    d_ref[TR + 1 : TR + 2] = line
    for f in range(3):
        for kr in range(3):
            for kc in range(3):
                at = (kr * 3 + f) * 16
                we_ref[at : at + 16, kc * C : (kc + 1) * C] = ew_ref[f, kr, kc]
    gather_body(pos_ref[1], tok_ref, before_ref, after_ref, cache_ref, x_ref, t_ref, lat_ref, old_ref)
    for g in range(STEPS):
        base = g * rows * WIDE
        taps = [x_ref[base + k * WIDE : base + (k + rows) * WIDE, 0:48] for k in range(3)]
        part = jnp.dot(jnp.concatenate(taps, axis=1), we_ref[...], preferred_element_type=F32)
        part = part.reshape(rows, TC + 2, VID, 3 * C)
        entry = part[:, 0:TC, :, 0:C] + part[:, 1 : TC + 1, :, C : 2 * C] + part[:, 2 : TC + 2, :, 2 * C :]
        entry = entry.reshape(m, C).astype(BF)
        if g == 0:
            load_wt.wait()
        loads[g].wait()
        stacked = jnp.concatenate([cm_ref[g * m : (g + 1) * m, :], entry], axis=1)
        out = jnp.dot(stacked, wt_ref[...], preferred_element_type=F32)
        out = out.reshape(rows, TC, 1, VID, 2 * C)
        out = jnp.concatenate([out[..., :C], out[..., C:]], axis=2)
        d_ref[1 + g * rows : 1 + (g + 1) * rows, 1 : TC + 1] = out.reshape(rows, TC, 2 * VID, C).astype(BF)


def mix(pos, tok, before, after, cache, ew, cm, wt):
    args = [held(v) for v in (tok, before, after, cache, ew)]
    hbm = pl.BlockSpec(memory_space=pltpu.HBM)
    return pl.pallas_call(
        mix_body,
        in_specs=[pl.BlockSpec(memory_space=pltpu.SMEM)] + [VM] * len(args) + [hbm, hbm],
        out_specs=VM,
        out_shape=pltpu.VMEM((TR + 2, TC + 2, 2 * VID, C), BF),
        scratch_shapes=[
            pltpu.VMEM((12 * WIDE, 128), BF),
            pltpu.VMEM((2, 6 * PITCH + 8, 128), F32),
            pltpu.VMEM((12 * WIDE, 128), F32),
            pltpu.VMEM((12 * WIDE, 128), F32),
            pltpu.VMEM((144, 3 * C), BF),
            pltpu.VMEM((TR * TC * VID, 2 * C), BF),
            pltpu.VMEM((3 * C, 2 * C), BF),
            pltpu.SemaphoreType.DMA((STEPS + 1,)),
        ],
        compiler_params=LIMIT,
        cost_estimate=pl.CostEstimate(flops=2 * 60000 * 65536, bytes_accessed=1 << 16, transcendentals=0),
        name="mix",
    )(pos, *args, cm, wt)


def fold_body(ut_ref, w_ref):
    def sums(get):
        return (get(0), get(1) + get(2)), (get(0) + get(1), get(2))

    rows = [sums(lambda r: ut_ref[r, c].astype(F32)) for c in range(3)]
    for a in range(2):
        for kr in range(2):
            cols = sums(lambda c: rows[c][a][kr])
            for b in range(2):
                for kc in range(2):
                    w = cols[b][kc].astype(BF)
                    at = (kr * 2 + kc) * C
                    w_ref[2 * a + b, 0:U, at : at + C] = w
                    w_ref[2 * a + b, U:256, at : at + C] = w[0:64]


def fold(ut):
    return call(fold_body, "fold", pltpu.VMEM((4, 256, 4 * C), BF), (ut,), 1 << 24)


def phase(d_ref, w_ref, gain, areas, a, b):
    parts, cells = [], 0
    for i0, ni, j0, nj in areas:
        taps = [
            d_ref[i0 + a + kr : i0 + a + kr + ni, j0 + b + kc : j0 + b + kc + nj].reshape(ni * nj * 2 * VID, C)
            for kr in range(2)
            for kc in range(2)
        ]
        parts.append(jnp.concatenate(taps, axis=1))
        cells += ni * nj
    full = jnp.concatenate(parts, axis=0) if len(parts) > 1 else parts[0]
    res = lax.dot_general(full, w_ref[2 * a + b], NT, preferred_element_type=F32)
    res = res.reshape(cells, 2, VID, 256)
    one = res[:, 0].reshape(cells * VID, 256)
    two = res[:, 1].reshape(cells * VID, 256)
    low = lax.broadcasted_iota(jnp.int32, (1, 128), 1) < 64
    o0 = one[:, :128]
    o1 = jnp.where(low, one[:, 128:], two[:, 128:])
    o2 = jnp.where(low, two[:, 128:], two[:, :128])
    q1 = o1 * o1
    s0 = jnp.sum(o0 * o0 + jnp.where(low, q1, 0.0), axis=1, keepdims=True)
    s1 = jnp.sum(o2 * o2 + jnp.where(low, 0.0, q1), axis=1, keepdims=True)
    r0 = lax.rsqrt(s0 * (1.0 / U) + EPSILON)
    r1 = lax.rsqrt(s1 * (1.0 / U) + EPSILON)
    o2 = pltpu.roll(o2, 64, 1)
    outs = []
    for k, (o, r) in enumerate(((o0, r0), (o1, jnp.where(low, r0, r1)), (o2, r1))):
        h = o * r * gain[:, 128 * k : 128 * (k + 1)]
        outs.append(h + h * jnp.tanh(h))
    return jnp.concatenate(outs, axis=1)


def both(d_ref, w_ref, gain, areas, a):
    n = sum(area[1] * area[3] for area in areas)
    outs = [phase(d_ref, w_ref, gain, areas, a, b).reshape(n, 1, VID, 2 * U) for b in range(2)]
    return jnp.concatenate(outs, axis=1).reshape(n, 2 * VID, 2 * U).astype(BF)


def half_gain(gain_ref):
    return jnp.concatenate([gain_ref[...], gain_ref[...]], axis=1) * 0.5


def sides_body(d_ref, w_ref, gain_ref, left_ref, right_ref):
    gain = half_gain(gain_ref)
    for a in range(2):
        v = both(d_ref, w_ref, gain, ((0, TR, 0, 1), (0, TR, TC - 1, 1)), a)
        left_ref[:, a] = v[:TR]
        right_ref[:, a] = v[TR:]


def sides(d, w, gain):
    side = jax.ShapeDtypeStruct((TR, 2, 2 * VID, 2 * U), BF)
    return call(sides_body, "sides", (side, side), (d, w, gain), 2 * 320 * 24 * 65536)


def strips_body(d_ref, w_ref, gain_ref, fl_ref, fr_ref, done_ref, top_ref, low_ref):
    del done_ref
    gain = half_gain(gain_ref)
    n = TC - 2
    for a in range(2):
        v = both(d_ref, w_ref, gain, ((0, 1, 1, n), (TR - 1, 1, 1, n)), a)
        top_ref[a, 1 : n + 1] = v[:n]
        low_ref[a, 1 : n + 1] = v[n:]
        for ref, i in ((top_ref, 0), (low_ref, TR - 1)):
            ref[a, 0] = fl_ref[i, a]
            ref[a, n + 1] = fr_ref[i, a]


def strips(d, w, gain, fl, fr, done):
    strip = jax.ShapeDtypeStruct((2, TC, 2 * VID, 2 * U), BF)
    return call(strips_body, "strips", (strip, strip), (d, w, gain, fl, fr, done), 2 * 832 * 24 * 65536)


FIRST, SPLIT = 3, 7


def upper_body(d_ref, w_ref, gain_ref, o_ref, *, start, stop):
    gain = half_gain(gain_ref)
    for i in range(start, stop):
        for a in range(2):
            o_ref[2 * (i - start) + a] = both(d_ref, w_ref, gain, ((i + 1, 1, 1, TC - 2),), a)


def upper(d, w, gain, start, stop):
    out = pltpu.VMEM((2 * (stop - start), TC - 2, 2 * VID, 2 * U), BF)
    body = functools.partial(upper_body, start=start, stop=stop)
    return call(body, "upper%d" % start, out, (d, w, gain), 2 * (stop - start) * 416 * 24 * 65536)


def ramp(pos, table_ref, amount, place):
    step = table_ref[jnp.clip(pos, 1, amount - 1)].astype(F32)
    sloped = jnp.clip(jnp.full((1, 1), place + 0.5, F32) / jnp.full((1, 1), step, F32) + 0.5, 0.0, 1.0)
    return jnp.where(pos <= 0, 1.0, jnp.where(pos >= amount, 0.0, sloped))


GROUP = 2


def lower_body(
    pos_ref, rr_ref, cr_ref, d_ref, w_ref, gain_ref, u_ref, v_ref, fl_ref, fr_ref, top_ref, low_ref, o_ref, a_ref, buf, sem
):
    gain = half_gain(gain_ref)
    for i in range(1 + SPLIT, TR - 1):
        for a in range(2):
            a_ref[2 * (i - 1 - SPLIT) + a] = both(d_ref, w_ref, gain, ((i, 1, 1, TC - 2),), a)
    r, c = pos_ref[0], pos_ref[1]
    up = [ramp(r, rr_ref, ROWS, p) for p in (0, 1)]
    down = [ramp(r + 1, rr_ref, ROWS, p) for p in (-2, -1)]
    groups = (TC - 2) // GROUP

    def sends(g):
        at = pl.ds(g * 2 * GROUP, 2 * GROUP)
        return pltpu.make_async_copy(buf.at[:, at], o_ref.at[:, at], sem.at[g])

    def put(j, rows):
        v = jnp.swapaxes(rows, 0, 1)
        for b in range(2):
            buf[:, 2 * j + b] = v[VID * b : VID * (b + 1)]

    def rows_of(j, k):
        if k < 2 * FIRST:
            return u_ref[k, j]
        return v_ref[k - 2 * FIRST, j] if k < 2 * SPLIT else a_ref[k - 2 * SPLIT, j]

    def inner(j):
        rows = []
        for p in range(16):
            v = rows_of(j, p)
            if p < 2:
                v = (v.astype(F32) * up[p] + top_ref[p, j + 1].astype(F32) * (1.0 - up[p])).astype(BF)
            elif p > 13:
                w = down[p - 14]
                v = (v.astype(F32) * (1.0 - w) + low_ref[p - 14, j + 1].astype(F32) * w).astype(BF)
            rows.append(v[None])
        put(j, jnp.concatenate(rows, axis=0))

    def outer(j, side_ref, slot, w):
        first = lax.broadcasted_iota(jnp.int32, (2 * VID, 1), 0) < VID
        w = jnp.where(first, w[0], w[1])

        def across(own, other):
            return own.astype(F32) * (1.0 - w) + other.astype(F32) * w

        rows = []
        for p in range(16):
            v = across(rows_of(j, p), side_ref[1 + p // 2, p % 2])
            if p < 2:
                v = v * up[p] + across(top_ref[p, j + 1], top_ref[p, slot]) * (1.0 - up[p])
            elif p > 13:
                k = down[p - 14]
                v = v * (1.0 - k) + across(low_ref[p - 14, j + 1], low_ref[p - 14, slot]) * k
            rows.append(v.astype(BF)[None])
        put(j, jnp.concatenate(rows, axis=0))

    outer(0, fl_ref, 0, [1.0 - ramp(c, cr_ref, COLS, x) for x in (0, 1)])
    for j in range(1, GROUP):
        inner(j)
    sends(0).start()

    def step(g, carry):
        for j in range(GROUP):
            inner(g * GROUP + j)
        sends(g).start()
        return carry

    lax.fori_loop(1, groups - 1, step, 0)
    for j in range(TC - 2 - GROUP, TC - 3):
        inner(j)
    outer(TC - 3, fr_ref, TC - 1, [ramp(c + 1, cr_ref, COLS, x) for x in (-2, -1)])
    sends(groups - 1).start()
    for g in range(groups):
        sends(g).wait()


def lower(pos, row_ramp, col_ramp, d, w, gain, u, v, fl, fr, top, low):
    out = jax.ShapeDtypeStruct((VID, 2 * (TC - 2), 16, 2 * U), BF)
    n = TR - 2 - SPLIT
    return call(
        lower_body,
        "lower",
        out,
        (pos, row_ramp, col_ramp, d, w, gain, u, v, fl, fr, top, low),
        2 * n * 416 * 24 * 65536,
        scratch=[
            pltpu.VMEM((2 * n, TC - 2, 2 * VID, 2 * U), BF),
            pltpu.VMEM((VID, 2 * (TC - 2), 16, 2 * U), BF),
            pltpu.SemaphoreType.DMA(((TC - 2) // GROUP,)),
        ],
        out_specs=pl.BlockSpec(memory_space=pltpu.HBM),
        smem=3,
    )


def per_device(
    latent_tokens,
    cache_latent,
    cache_middle,
    entry_weight,
    time_weight,
    up_weight,
    norm_gain,
    row_ramp,
    col_ramp,
):
    row_pos = lax.axis_index("rows")
    col_pos = lax.axis_index("cols")
    tok = jnp.transpose(latent_tokens, (0, 2, 1))
    before = shift(tok[:, :, 156:], "rows", 1)
    after = shift(tok[:, :, :52], "rows", -1)
    cache = jnp.transpose(cache_latent, (0, 1, 2, 4, 3))
    cm = jnp.transpose(cache_middle, (2, 3, 0, 1, 4)).reshape(TR * TC * VID, 2 * C)
    wt = time_weight.reshape(3 * C, 2 * C)
    ut = jnp.transpose(up_weight, (0, 1, 3, 2))
    gain = norm_gain.reshape(1, U)
    pos = jnp.stack([row_pos, col_pos]).astype(jnp.int32)
    w = fold(ut)
    d = mix(pos, tok, before, after, cache, entry_weight, cm, wt)
    left, right = sides(d, w, gain)
    from_left = shift(right, "cols", 1)
    from_right = shift(left, "cols", -1)
    u = upper(d, w, gain, 0, FIRST)
    top, low = strips(d, w, gain, from_left, from_right, u)
    from_above = shift(low, "rows", 1)
    from_below = shift(top, "rows", -1)
    v = upper(d, w, gain, FIRST, SPLIT)
    out = lower(pos, row_ramp, col_ramp, d, w, gain, u, v, from_left, from_right, from_above, from_below)
    return jnp.transpose(out, (0, 2, 1, 3))


def solution(mesh):
    in_specs = (
        P(None, "rows", None),
        P(None, None, "rows", "cols", None),
        P(None, None, "rows", "cols", None),
        P(),
        P(),
        P(),
        P(),
        P(),
        P(),
    )
    out_specs = P(None, "rows", "cols", None)
    return jax.shard_map(
        per_device, mesh=mesh, in_specs=in_specs, out_specs=out_specs, check_vma=False
    )
```

profile of v0, /device:TPU:25, one launch (start us, length us, event | category | flops | bytes accessed | tf_op | source)
XLA Modules:
  0.0 66.0 jit_solution(2522255970760620115)
XLA Ops:
  0.0 1.1 %fusion = (bf16[8,64,52]{2,1,0:T(8,128)(2,1)S(1)}, bf16[8,64,52]{2,1,0:T(8,128)(2,1)S(1)}) fusion(bf16[8,64,208]{2,1,0:T(8,128)(2,1)} %bitcast.12), kind=kLoop, calls=%fused_computation.1 | loop fusion | bytes 212992 | tf_op jit(solution)/shard_map/slice | solution.py:393
  1.1 2.6 %collective-permute-start.1 = (bf16[8,64,52]{2,1,0:T(8,128)(2,1)S(1)}, bf16[8,64,52]{2,1,0:T(8,128)(2,1)S(1)}, u32[]{:S(2)}, u32[]{:S(2)}) collective-permute-start(bf16[8,64,52]{2,1,0:T(8,128)(2,1)S(1)} %get-tuple-element.13), channel_id=1, source_target_pairs={{4,0},{8,4},{12,8},{16,12},{20,16},{24,20},{28,24},{32,28},{36,32}... | collective-permute-start | bytes 159752 | tf_op jit(solution)/shard_map/ppermute | solution.py:22
  3.7 5.1 %collective-permute-start = (bf16[8,64,52]{2,1,0:T(8,128)(2,1)S(1)}, bf16[8,64,52]{2,1,0:T(8,128)(2,1)S(1)}, u32[]{:S(2)}, u32[]{:S(2)}) collective-permute-start(bf16[8,64,52]{2,1,0:T(8,128)(2,1)S(1)} %get-tuple-element.14), channel_id=1, source_target_pairs={{0,4},{4,8},{8,12},{12,16},{16,20},{20,24},{24,28},{28,32},{32,36}... | collective-permute-start | bytes 159752 | tf_op jit(solution)/shard_map/ppermute | solution.py:22
  8.8 0.1 pad_add_fusion.pos_ref
  8.8 0.0 copy-start
  8.8 3.3 %copy.10 = bf16[10,28,8,2,384]{4,2,3,1,0:T(8,128)(2,1)S(1)} copy(bf16[10,28,8,2,384]{4,3,1,0,2:T(2,128)(2,1)} %bitcast.21) | data formatting | bytes 6881280 | tf_op jit(solution)/shard_map/transpose | solution.py:395
  12.2 0.0 copy-start.1
  12.2 0.0 copy-start.5
  12.2 0.0 copy-start.6
  12.2 0.0 copy-start.7
  12.2 0.0 copy-done
  12.2 0.6 fold.1.w_ref
  12.8 0.0 collective-permute-done.1.after_ref
  12.8 0.0 collective-permute-done.before_ref
  12.8 0.3 copy-done.1
  13.1 0.6 copy-done.5
  13.7 0.1 copy-done.6
  13.9 0.1 copy-done.7
  13.9 0.0 copy-start.2
  13.9 11.5 %mix.1.d_ref = bf16[12,30,16,384]{3,2,1,0:T(8,128)(2,1)S(1)} custom-call(s32[2]{0:T(128)S(1)} %pad_add_fusion.pos_ref, bf16[8,64,208]{2,1,0:T(8,128)(2,1)S(1)} %bitcast.13, bf16[8,64,52]{2,1,0:T(8,128)(2,1)S(1)} %collective-permute-done.before_ref, bf16[8,64,52]{2,1,0:T(8,128)(2,1)S(1)} %collective-permute-done.1.after_ref, ...), custom_call_target="tpu_custom_call" | custom-call | flops 7864320000 | bytes 65536 | tf_op jit(solution)/shard_map/mix/pallas_call | solution.py:144
  25.5 0.0 copy-done.2
  25.5 1.6 %sides.1 = (bf16[10,2,16,384]{3,2,1,0:T(8,128)(2,1)S(1)}, bf16[10,2,16,384]{3,2,1,0:T(8,128)(2,1)S(1)}) custom-call(bf16[12,30,16,384]{3,2,1,0:T(8,128)(2,1)S(1)} %mix.1.d_ref, bf16[4,256,1536]{2,1,0:T(8,128)(2,1)S(1)} %fold.1.w_ref, f32[1,192]{1,0:T(1,128)S(1)} %bitcast.14), custom_call_target="tpu_custom_call" | custom-call | flops 1006632960 | bytes 65536 | tf_op jit(solution)/shard_map/sides/pallas_call | solution.py:36
  27.1 3.6 %collective-permute-start.2 = (bf16[10,2,16,384]{3,2,1,0:T(8,128)(2,1)S(1)}, bf16[10,2,16,384]{3,2,1,0:T(8,128)(2,1)S(1)}, u32[]{:S(2)}, u32[]{:S(2)}) collective-permute-start(bf16[10,2,16,384]{3,2,1,0:T(8,128)(2,1)S(1)} %get-tuple-element.9), channel_id=1, source_target_pairs={{0,1},{1,2},{2,3},{4,5},{5,6},{6,7},{8,9},{9,10},{10,11},{12,13},{... | collective-permute-start | bytes 737288 | tf_op jit(solution)/shard_map/ppermute | solution.py:22
  30.6 1.5 %collective-permute-start.3 = (bf16[10,2,16,384]{3,2,1,0:T(8,128)(2,1)S(1)}, bf16[10,2,16,384]{3,2,1,0:T(8,128)(2,1)S(1)}, u32[]{:S(2)}, u32[]{:S(2)}) collective-permute-start(bf16[10,2,16,384]{3,2,1,0:T(8,128)(2,1)S(1)} %get-tuple-element.10), channel_id=1, source_target_pairs={{1,0},{2,1},{3,2},{5,4},{6,5},{7,6},{9,8},{10,9},{11,10},{13,12},{... | collective-permute-start | bytes 737288 | tf_op jit(solution)/shard_map/ppermute | solution.py:22
  32.1 4.7 %upper0.1.done_ref.u_ref = bf16[6,26,16,384]{3,2,1,0:T(8,128)(2,1)S(1)} custom-call(bf16[12,30,16,384]{3,2,1,0:T(8,128)(2,1)S(1)} %mix.1.d_ref, bf16[4,256,1536]{2,1,0:T(8,128)(2,1)S(1)} %fold.1.w_ref, f32[1,192]{1,0:T(1,128)S(1)} %bitcast.15), custom_call_target="tpu_custom_call" | custom-call | flops 3925868544 | bytes 65536 | tf_op jit(solution)/shard_map/upper0/pallas_call | solution.py:36
  36.8 0.0 collective-permute-done.2.fl_ref
  36.8 1.5 %collective-permute-done.3.fr_ref = bf16[10,2,16,384]{3,2,1,0:T(8,128)(2,1)S(1)} collective-permute-done((bf16[10,2,16,384]{3,2,1,0:T(8,128)(2,1)S(1)}, bf16[10,2,16,384]{3,2,1,0:T(8,128)(2,1)S(1)}, u32[]{:S(2)}, u32[]{:S(2)}) %collective-permute-start.3) | collective-permute-done | bytes 245792 | tf_op jit(solution)/shard_map/ppermute | solution.py:22
  38.3 3.7 %strips.1 = (bf16[2,28,16,384]{3,2,1,0:T(8,128)(2,1)S(1)}, bf16[2,28,16,384]{3,2,1,0:T(8,128)(2,1)S(1)}) custom-call(bf16[12,30,16,384]{3,2,1,0:T(8,128)(2,1)S(1)} %mix.1.d_ref, bf16[4,256,1536]{2,1,0:T(8,128)(2,1)S(1)} %fold.1.w_ref, f32[1,192]{1,0:T(1,128)S(1)} %bitcast.16, bf16[10,2,16,384]{3,2,1,0:T(8,128)(2,1)S(1)} %collective-permute-done.2.fl_ref, ...), custom_call_target="tpu_custom_call" | custom-call | flops 2617245696 | bytes 65536 | tf_op jit(solution)/shard_map/strips/pallas_call | solution.py:36
  42.0 4.0 %collective-permute-start.4 = (bf16[2,28,16,384]{3,2,1,0:T(8,128)(2,1)S(1)}, bf16[2,28,16,384]{3,2,1,0:T(8,128)(2,1)S(1)}, u32[]{:S(2)}, u32[]{:S(2)}) collective-permute-start(bf16[2,28,16,384]{3,2,1,0:T(8,128)(2,1)S(1)} %get-tuple-element.11), channel_id=1, source_target_pairs={{0,4},{4,8},{8,12},{12,16},{16,20},{20,24},{24,28},{28,32},{32,36}... | collective-permute-start | bytes 2064392 | tf_op jit(solution)/shard_map/ppermute | solution.py:22
  45.9 0.0 copy-start.3
  45.9 0.0 copy-start.4
  46.0 2.1 %collective-permute-start.5 = (bf16[2,28,16,384]{3,2,1,0:T(8,128)(2,1)S(1)}, bf16[2,28,16,384]{3,2,1,0:T(8,128)(2,1)S(1)}, u32[]{:S(2)}, u32[]{:S(2)}) collective-permute-start(bf16[2,28,16,384]{3,2,1,0:T(8,128)(2,1)S(1)} %get-tuple-element.12), channel_id=1, source_target_pairs={{4,0},{8,4},{12,8},{16,12},{20,16},{24,20},{28,24},{32,28},{36,32}... | collective-permute-start | bytes 2064392 | tf_op jit(solution)/shard_map/ppermute | solution.py:22
  48.1 6.0 %upper3.1.v_ref = bf16[8,26,16,384]{3,2,1,0:T(8,128)(2,1)S(1)} custom-call(bf16[12,30,16,384]{3,2,1,0:T(8,128)(2,1)S(1)} %mix.1.d_ref, bf16[4,256,1536]{2,1,0:T(8,128)(2,1)S(1)} %fold.1.w_ref, f32[1,192]{1,0:T(1,128)S(1)} %bitcast.17), custom_call_target="tpu_custom_call" | custom-call | flops 5234491392 | bytes 65536 | tf_op jit(solution)/shard_map/upper3/pallas_call | solution.py:36
  54.1 0.0 collective-permute-done.4.top_ref
  54.1 6.2 %collective-permute-done.5.low_ref = bf16[2,28,16,384]{3,2,1,0:T(8,128)(2,1)S(1)} collective-permute-done((bf16[2,28,16,384]{3,2,1,0:T(8,128)(2,1)S(1)}, bf16[2,28,16,384]{3,2,1,0:T(8,128)(2,1)S(1)}, u32[]{:S(2)}, u32[]{:S(2)}) %collective-permute-start.5) | collective-permute-done | bytes 688160 | tf_op jit(solution)/shard_map/ppermute | solution.py:22
  60.3 0.0 copy-done.3
  60.3 0.0 copy-done.4
  60.3 5.5 %lower.1 = bf16[8,52,16,384]{3,2,1,0:T(8,128)(2,1)} custom-call(s32[2]{0:T(128)S(1)} %pad_add_fusion.pos_ref, s32[32]{0:T(128)S(1)} %copy-done.3, s32[4]{0:T(128)S(1)} %copy-done.4, bf16[12,30,16,384]{3,2,1,0:T(8,128)(2,1)S(1)} %mix.1.d_ref, bf16[4,256,1536]{2,1,0:T(8,128)(2,1)S(1)} %fold.1.w_ref, f32[1,192]{1,0:T(1,128)S(1)} %bitcast.18, ...), custom_call_target="tpu_custom_call" | custom-call | flops 1308622848 | bytes 65536 | tf_op jit(solution)/shard_map/lower/pallas_call | solution.py:36
Async XLA Ops:
  1.1 11.7 %collective-permute-start.1 = (bf16[8,64,52]{2,1,0:T(8,128)(2,1)S(1)}, bf16[8,64,52]{2,1,0:T(8,128)(2,1)S(1)}, u32[]{:S(2)}, u32[]{:S(2)}) collective-permute-start(bf16[8,64,52]{2,1,0:T(8,128)(2,1)S(1)} %get-tuple-element.13), channel_id=1, source_target_pairs={{4,0},{8,4},{12,8},{16,12},{20,16},{24,20},{28,24},{32,28},{36,32}... | collective-permute-start | bytes 159752 | tf_op jit(solution)/shard_map/ppermute | solution.py:22
  3.7 9.1 %collective-permute-start = (bf16[8,64,52]{2,1,0:T(8,128)(2,1)S(1)}, bf16[8,64,52]{2,1,0:T(8,128)(2,1)S(1)}, u32[]{:S(2)}, u32[]{:S(2)}) collective-permute-start(bf16[8,64,52]{2,1,0:T(8,128)(2,1)S(1)} %get-tuple-element.14), channel_id=1, source_target_pairs={{0,4},{4,8},{8,12},{12,16},{16,20},{20,24},{24,28},{28,32},{32,36}... | collective-permute-start | bytes 159752 | tf_op jit(solution)/shard_map/ppermute | solution.py:22
  8.8 3.4 %copy-start = (bf16[3,3,384,192]{2,3,1,0:T(8,128)(2,1)S(1)}, bf16[3,3,384,192]{2,3,1,0:T(8,128)(2,1)}, u32[]{:S(2)}) copy-start(bf16[3,3,384,192]{2,3,1,0:T(8,128)(2,1)} %param.14) | copy-start | bytes 3981316
  12.2 1.0 %copy-start.1 = (bf16[8,208,64]{1,2,0:T(8,128)(2,1)S(1)}, bf16[8,208,64]{1,2,0:T(8,128)(2,1)}, u32[]{:S(2)}) copy-start(bf16[8,208,64]{1,2,0:T(8,128)(2,1)} %param.9) | copy-start | bytes 638980
  12.2 1.6 %copy-start.5 = (bf16[3,384,768]{2,1,0:T(8,128)(2,1)S(1)}, bf16[3,384,768]{2,1,0:T(8,128)(2,1)}, u32[]{:S(2)}) copy-start(bf16[3,384,768]{2,1,0:T(8,128)(2,1)} %param.13) | copy-start | bytes 5308420
  12.2 1.7 %copy-start.6 = (bf16[8,2,10,28,16]{3,4,2,1,0:T(8,128)(2,1)S(1)}, bf16[8,2,10,28,16]{3,4,2,1,0:T(8,128)(2,1)}, u32[]{:S(2)}) copy-start(bf16[8,2,10,28,16]{3,4,2,1,0:T(8,128)(2,1)} %param.10) | copy-start | bytes 430084
  12.2 1.8 %copy-start.7 = (bf16[3,3,3,16,384]{4,3,2,1,0:T(8,128)(2,1)S(1)}, bf16[3,3,3,16,384]{4,3,2,1,0:T(8,128)(2,1)}, u32[]{:S(2)}) copy-start(bf16[3,3,3,16,384]{4,3,2,1,0:T(8,128)(2,1)} %ew_ref.1) | copy-start | bytes 995332
  13.9 11.5 %copy-start.2 = (f32[192]{0:T(256)S(1)}, f32[192]{0:T(256)}, u32[]{:S(2)}) copy-start(f32[192]{0:T(256)} %param.15) | copy-start | bytes 2308
  27.1 9.7 %collective-permute-start.2 = (bf16[10,2,16,384]{3,2,1,0:T(8,128)(2,1)S(1)}, bf16[10,2,16,384]{3,2,1,0:T(8,128)(2,1)S(1)}, u32[]{:S(2)}, u32[]{:S(2)}) collective-permute-start(bf16[10,2,16,384]{3,2,1,0:T(8,128)(2,1)S(1)} %get-tuple-element.9), channel_id=1, source_target_pairs={{0,1},{1,2},{2,3},{4,5},{5,6},{6,7},{8,9},{9,10},{10,11},{12,13},{... | collective-permute-start | bytes 737288 | tf_op jit(solution)/shard_map/ppermute | solution.py:22
  30.6 7.6 %collective-permute-start.3 = (bf16[10,2,16,384]{3,2,1,0:T(8,128)(2,1)S(1)}, bf16[10,2,16,384]{3,2,1,0:T(8,128)(2,1)S(1)}, u32[]{:S(2)}, u32[]{:S(2)}) collective-permute-start(bf16[10,2,16,384]{3,2,1,0:T(8,128)(2,1)S(1)} %get-tuple-element.10), channel_id=1, source_target_pairs={{1,0},{2,1},{3,2},{5,4},{6,5},{7,6},{9,8},{10,9},{11,10},{13,12},{... | collective-permute-start | bytes 737288 | tf_op jit(solution)/shard_map/ppermute | solution.py:22
  42.0 12.2 %collective-permute-start.4 = (bf16[2,28,16,384]{3,2,1,0:T(8,128)(2,1)S(1)}, bf16[2,28,16,384]{3,2,1,0:T(8,128)(2,1)S(1)}, u32[]{:S(2)}, u32[]{:S(2)}) collective-permute-start(bf16[2,28,16,384]{3,2,1,0:T(8,128)(2,1)S(1)} %get-tuple-element.11), channel_id=1, source_target_pairs={{0,4},{4,8},{8,12},{12,16},{16,20},{20,24},{24,28},{28,32},{32,36}... | collective-permute-start | bytes 2064392 | tf_op jit(solution)/shard_map/ppermute | solution.py:22
  45.9 14.4 %copy-start.3 = (s32[32]{0:T(128)S(1)}, s32[32]{0:T(128)}, u32[]{:S(2)}) copy-start(s32[32]{0:T(128)} %rr_ref.1) | copy-start | bytes 388
  45.9 14.4 %copy-start.4 = (s32[4]{0:T(128)S(1)}, s32[4]{0:T(128)}, u32[]{:S(2)}) copy-start(s32[4]{0:T(128)} %cr_ref.1) | copy-start | bytes 52
  46.0 14.4 %collective-permute-start.5 = (bf16[2,28,16,384]{3,2,1,0:T(8,128)(2,1)S(1)}, bf16[2,28,16,384]{3,2,1,0:T(8,128)(2,1)S(1)}, u32[]{:S(2)}, u32[]{:S(2)}) collective-permute-start(bf16[2,28,16,384]{3,2,1,0:T(8,128)(2,1)S(1)} %get-tuple-element.12), channel_id=1, source_target_pairs={{4,0},{8,4},{12,8},{16,12},{20,16},{24,20},{28,24},{32,28},{36,32}... | collective-permute-start | bytes 2064392 | tf_op jit(solution)/shard_map/ppermute | solution.py:22
where the time goes:
time: 66.3 us; the launch traced here: 66 us
  Pallas kernels  33.5 us (51%)
  starting transfers between devices  18.8 us (28%)
  waiting for transfers between devices  7.66 us (12%)
  local copies, waits for them, and re-layouts  5.56 us (8%)
    pallas_call x6, Pallas kernels, call(): pl.pallas_call(body, in_specs=specs, out_specs=jax.tree.map(lambda _: VM,...  22 us
    ppermute x6, starting transfers between devices, shift(): return lax.ppermute(value, axis, pairs)  18.8 us
    pallas_call x1, Pallas kernels, mix(): pl.pallas_call(mix_body, in_specs=[pl.BlockSpec(memory_space=pltpu.SMEM)]...  11.5 us
    ppermute x6, waiting for transfers between devices, shift(): return lax.ppermute(value, axis, pairs)  7.66 us
    transpose x1, local copies, waits for them, and re-layouts, per_device(): jnp.transpose(cache_middle, (2, 3, 0, 1, 4)).reshape(TR * TC * VID, 2 * C)  3.3 us
  transfers between devices with their start and end apart: 6, of which 2 were waited for; matrix products, arithmetic and copies ran while one was open for 5% of the time, Pallas kernels for 17%

commit v1 on v0

--- a/solution.py
+++ b/solution.py
@@ -80,86 +80,105 @@
     x_ref[...] = jnp.where(lane < 32, old_ref[...], jnp.where(lane < 48, lat_ref[...], 0.0)).astype(BF)
 
 
-def mix_body(
+def mixed(x_ref, we_ref, cm_ref, wt_ref, areas):
+    taps, olds, sizes = [], [], []
+    for r0, nr, c0, nc in areas:
+        for t in range(r0, r0 + nr):
+            wide = (nc + 2) * VID
+            at = [(t + k) * WIDE + c0 * VID for k in range(3)]
+            taps.append(jnp.concatenate([x_ref[p : p + wide, 0:48] for p in at], axis=1))
+            p = (t * TC + c0) * VID
+            olds.append(cm_ref[p : p + nc * VID, :])
+            sizes.append(nc)
+    part = jnp.dot(jnp.concatenate(taps, axis=0), we_ref[...], preferred_element_type=F32)
+    part = part.reshape(-1, VID, 3 * C)
+    entry, at = [], 0
+    for nc in sizes:
+        three = [part[at + k : at + k + nc, :, k * C : (k + 1) * C] for k in range(3)]
+        entry.append(three[0] + three[1] + three[2])
+        at += nc + 2
+    cells = sum(sizes)
+    entry = jnp.concatenate(entry, axis=0).reshape(cells * VID, C).astype(BF)
+    stacked = jnp.concatenate([jnp.concatenate(olds, axis=0), entry], axis=1)
+    out = jnp.dot(stacked, wt_ref[...], preferred_element_type=F32).reshape(cells, 1, VID, 2 * C)
+    out = jnp.concatenate([out[..., :C], out[..., C:]], axis=1)
+    return out.reshape(cells, 2 * VID, C).astype(BF)
+
+
+def edge_body(
     pos_ref,
     tok_ref,
     before_ref,
     after_ref,
     cache_ref,
     ew_ref,
-    cm_hbm,
-    wt_hbm,
-    d_ref,
+    cm_ref,
+    wt_ref,
+    w_ref,
+    gain_ref,
     x_ref,
+    we_ref,
+    dl_ref,
+    dr_ref,
+    left_ref,
+    right_ref,
     t_ref,
     lat_ref,
     old_ref,
-    we_ref,
-    cm_ref,
-    wt_ref,
-    sem,
 ):
-    rows = TR // STEPS
-    m = rows * TC * VID
-    loads = [
-        pltpu.make_async_copy(cm_hbm.at[pl.ds(g * m, m)], cm_ref.at[pl.ds(g * m, m)], sem.at[g]) for g in range(STEPS)
-    ]
-    load_wt = pltpu.make_async_copy(wt_hbm, wt_ref, sem.at[STEPS])
-    loads[0].start()
-    load_wt.start()
-    for load in loads[1:]:
-        load.start()
-    edge = jnp.zeros((TR + 2, 1, 2 * VID, C), BF)
-    d_ref[:, 0:1] = edge
-    d_ref[:, TC + 1 : TC + 2] = edge
-    line = jnp.zeros((1, TC + 2, 2 * VID, C), BF)
-    d_ref[0:1] = line
-    d_ref[TR + 1 : TR + 2] = line
+    dl_ref[...] = jnp.zeros(dl_ref.shape, BF)
+    dr_ref[...] = jnp.zeros(dr_ref.shape, BF)
     for f in range(3):
         for kr in range(3):
             for kc in range(3):
                 at = (kr * 3 + f) * 16
                 we_ref[at : at + 16, kc * C : (kc + 1) * C] = ew_ref[f, kr, kc]
     gather_body(pos_ref[1], tok_ref, before_ref, after_ref, cache_ref, x_ref, t_ref, lat_ref, old_ref)
-    for g in range(STEPS):
-        base = g * rows * WIDE
-        taps = [x_ref[base + k * WIDE : base + (k + rows) * WIDE, 0:48] for k in range(3)]
-        part = jnp.dot(jnp.concatenate(taps, axis=1), we_ref[...], preferred_element_type=F32)
-        part = part.reshape(rows, TC + 2, VID, 3 * C)
-        entry = part[:, 0:TC, :, 0:C] + part[:, 1 : TC + 1, :, C : 2 * C] + part[:, 2 : TC + 2, :, 2 * C :]
-        entry = entry.reshape(m, C).astype(BF)
-        if g == 0:
-            load_wt.wait()
-        loads[g].wait()
-        stacked = jnp.concatenate([cm_ref[g * m : (g + 1) * m, :], entry], axis=1)
-        out = jnp.dot(stacked, wt_ref[...], preferred_element_type=F32)
-        out = out.reshape(rows, TC, 1, VID, 2 * C)
-        out = jnp.concatenate([out[..., :C], out[..., C:]], axis=2)
-        d_ref[1 + g * rows : 1 + (g + 1) * rows, 1 : TC + 1] = out.reshape(rows, TC, 2 * VID, C).astype(BF)
-
-
-def mix(pos, tok, before, after, cache, ew, cm, wt):
-    args = [held(v) for v in (tok, before, after, cache, ew)]
-    hbm = pl.BlockSpec(memory_space=pltpu.HBM)
-    return pl.pallas_call(
-        mix_body,
-        in_specs=[pl.BlockSpec(memory_space=pltpu.SMEM)] + [VM] * len(args) + [hbm, hbm],
-        out_specs=VM,
-        out_shape=pltpu.VMEM((TR + 2, TC + 2, 2 * VID, C), BF),
-        scratch_shapes=[
-            pltpu.VMEM((12 * WIDE, 128), BF),
+    d = mixed(x_ref, we_ref, cm_ref, wt_ref, ((0, TR, 0, 2), (0, TR, TC - 2, 2)))
+    dl_ref[1 : TR + 1, 1:3] = d[: 2 * TR].reshape(TR, 2, 2 * VID, C)
+    dr_ref[1 : TR + 1, 0:2] = d[2 * TR :].reshape(TR, 2, 2 * VID, C)
+    gain = half_gain(gain_ref)
+    for a in range(2):
+        v = both(w_ref, gain, ((dl_ref, 0, TR, 0, 1), (dr_ref, 0, TR, 0, 1)), a)
+        left_ref[:, a] = v[:TR]
+        right_ref[:, a] = v[TR:]
+
+
+def edge(pos, tok, before, after, cache, ew, cm, wt, w, gain):
+    part = pltpu.VMEM((TR + 2, 3, 2 * VID, C), BF)
+    side = jax.ShapeDtypeStruct((TR, 2, 2 * VID, 2 * U), BF)
+    outs = (pltpu.VMEM((12 * WIDE, 128), BF), pltpu.VMEM((144, 3 * C), BF), part, part, side, side)
+    return call(
+        edge_body,
+        "edge",
+        outs,
+        (pos, tok, before, after, cache, ew, cm, wt, w, gain),
+        2 * 40000 * 65536,
+        scratch=[
             pltpu.VMEM((2, 6 * PITCH + 8, 128), F32),
             pltpu.VMEM((12 * WIDE, 128), F32),
             pltpu.VMEM((12 * WIDE, 128), F32),
-            pltpu.VMEM((144, 3 * C), BF),
-            pltpu.VMEM((TR * TC * VID, 2 * C), BF),
-            pltpu.VMEM((3 * C, 2 * C), BF),
-            pltpu.SemaphoreType.DMA((STEPS + 1,)),
         ],
-        compiler_params=LIMIT,
-        cost_estimate=pl.CostEstimate(flops=2 * 60000 * 65536, bytes_accessed=1 << 16, transcendentals=0),
-        name="mix",
-    )(pos, *args, cm, wt)
+        smem=1,
+    )
+
+
+def rest_body(x_ref, we_ref, cm_ref, wt_ref, dl_ref, dr_ref, d_ref):
+    n = TC - 4
+    line = jnp.zeros((1, n, 2 * VID, C), BF)
+    d_ref[0:1, 3 : n + 3] = line
+    d_ref[TR + 1 : TR + 2, 3 : n + 3] = line
+    d_ref[:, 0:3] = dl_ref[...]
+    d_ref[:, n + 3 : n + 6] = dr_ref[...]
+    rows = TR // STEPS
+    for g in range(STEPS):
+        d = mixed(x_ref, we_ref, cm_ref, wt_ref, ((g * rows, rows, 2, n),))
+        d_ref[1 + g * rows : 1 + (g + 1) * rows, 3 : n + 3] = d.reshape(rows, n, 2 * VID, C)
+
+
+def rest(x, we, cm, wt, dl, dr):
+    out = pltpu.VMEM((TR + 2, TC + 2, 2 * VID, C), BF)
+    return call(rest_body, "rest", out, (x, we, cm, wt, dl, dr), 2 * 45000 * 65536)
 
 
 def fold_body(ut_ref, w_ref):
@@ -182,9 +201,9 @@
     return call(fold_body, "fold", pltpu.VMEM((4, 256, 4 * C), BF), (ut,), 1 << 24)
 
 
-def phase(d_ref, w_ref, gain, areas, a, b):
+def phase(w_ref, gain, areas, a, b):
     parts, cells = [], 0
-    for i0, ni, j0, nj in areas:
+    for d_ref, i0, ni, j0, nj in areas:
         taps = [
             d_ref[i0 + a + kr : i0 + a + kr + ni, j0 + b + kc : j0 + b + kc + nj].reshape(ni * nj * 2 * VID, C)
             for kr in range(2)
@@ -214,9 +233,9 @@
     return jnp.concatenate(outs, axis=1)
 
 
-def both(d_ref, w_ref, gain, areas, a):
-    n = sum(area[1] * area[3] for area in areas)
-    outs = [phase(d_ref, w_ref, gain, areas, a, b).reshape(n, 1, VID, 2 * U) for b in range(2)]
+def both(w_ref, gain, areas, a):
+    n = sum(area[2] * area[4] for area in areas)
+    outs = [phase(w_ref, gain, areas, a, b).reshape(n, 1, VID, 2 * U) for b in range(2)]
     return jnp.concatenate(outs, axis=1).reshape(n, 2 * VID, 2 * U).astype(BF)
 
 
@@ -224,51 +243,45 @@
     return jnp.concatenate([gain_ref[...], gain_ref[...]], axis=1) * 0.5
 
 
-def sides_body(d_ref, w_ref, gain_ref, left_ref, right_ref):
-    gain = half_gain(gain_ref)
-    for a in range(2):
-        v = both(d_ref, w_ref, gain, ((0, TR, 0, 1), (0, TR, TC - 1, 1)), a)
-        left_ref[:, a] = v[:TR]
-        right_ref[:, a] = v[TR:]
-
-
-def sides(d, w, gain):
-    side = jax.ShapeDtypeStruct((TR, 2, 2 * VID, 2 * U), BF)
-    return call(sides_body, "sides", (side, side), (d, w, gain), 2 * 320 * 24 * 65536)
-
-
-def strips_body(d_ref, w_ref, gain_ref, fl_ref, fr_ref, done_ref, top_ref, low_ref):
-    del done_ref
+def strips_body(d_ref, w_ref, gain_ref, top_ref, low_ref):
     gain = half_gain(gain_ref)
     n = TC - 2
     for a in range(2):
-        v = both(d_ref, w_ref, gain, ((0, 1, 1, n), (TR - 1, 1, 1, n)), a)
-        top_ref[a, 1 : n + 1] = v[:n]
-        low_ref[a, 1 : n + 1] = v[n:]
-        for ref, i in ((top_ref, 0), (low_ref, TR - 1)):
+        v = both(w_ref, gain, ((d_ref, 0, 1, 1, n), (d_ref, TR - 1, 1, 1, n)), a)
+        top_ref[a] = v[:n]
+        low_ref[a] = v[n:]
+
+
+def strips(d, w, gain):
+    strip = pltpu.VMEM((2, TC - 2, 2 * VID, 2 * U), BF)
+    return call(strips_body, "strips", (strip, strip), (d, w, gain), 2 * 832 * 24 * 65536)
+
+
+def join_body(t_ref, l_ref, fl_ref, fr_ref, top_ref, low_ref):
+    n = TC - 2
+    for ref, own_ref, i in ((top_ref, t_ref, 0), (low_ref, l_ref, TR - 1)):
+        ref[:, 1 : n + 1] = own_ref[...]
+        for a in range(2):
             ref[a, 0] = fl_ref[i, a]
             ref[a, n + 1] = fr_ref[i, a]
 
 
-def strips(d, w, gain, fl, fr, done):
+def join(t, l, fl, fr):
     strip = jax.ShapeDtypeStruct((2, TC, 2 * VID, 2 * U), BF)
-    return call(strips_body, "strips", (strip, strip), (d, w, gain, fl, fr, done), 2 * 832 * 24 * 65536)
-
-
-FIRST, SPLIT = 3, 7
-
-
-def upper_body(d_ref, w_ref, gain_ref, o_ref, *, start, stop):
+    return call(join_body, "join", (strip, strip), (t, l, fl, fr), 1 << 20)
+
+
+def upper_body(d_ref, w_ref, gain_ref, after_ref, o_ref):
+    del after_ref
     gain = half_gain(gain_ref)
-    for i in range(start, stop):
+    for i in range(TR - 2):
         for a in range(2):
-            o_ref[2 * (i - start) + a] = both(d_ref, w_ref, gain, ((i + 1, 1, 1, TC - 2),), a)
-
-
-def upper(d, w, gain, start, stop):
-    out = pltpu.VMEM((2 * (stop - start), TC - 2, 2 * VID, 2 * U), BF)
-    body = functools.partial(upper_body, start=start, stop=stop)
-    return call(body, "upper%d" % start, out, (d, w, gain), 2 * (stop - start) * 416 * 24 * 65536)
+            o_ref[2 * i + a] = both(w_ref, gain, ((d_ref, i + 1, 1, 1, TC - 2),), a)
+
+
+def upper(d, w, gain, after):
+    out = pltpu.VMEM((2 * (TR - 2), TC - 2, 2 * VID, 2 * U), BF)
+    return call(upper_body, "upper", out, (d, w, gain, after), 2 * (TR - 2) * 416 * 24 * 65536)
 
 
 def ramp(pos, table_ref, amount, place):
@@ -280,13 +293,7 @@
 GROUP = 2
 
 
-def lower_body(
-    pos_ref, rr_ref, cr_ref, d_ref, w_ref, gain_ref, u_ref, v_ref, fl_ref, fr_ref, top_ref, low_ref, o_ref, a_ref, buf, sem
-):
-    gain = half_gain(gain_ref)
-    for i in range(1 + SPLIT, TR - 1):
-        for a in range(2):
-            a_ref[2 * (i - 1 - SPLIT) + a] = both(d_ref, w_ref, gain, ((i, 1, 1, TC - 2),), a)
+def lower_body(pos_ref, rr_ref, cr_ref, u_ref, fl_ref, fr_ref, top_ref, low_ref, o_ref, buf, sem):
     r, c = pos_ref[0], pos_ref[1]
     up = [ramp(r, rr_ref, ROWS, p) for p in (0, 1)]
     down = [ramp(r + 1, rr_ref, ROWS, p) for p in (-2, -1)]
@@ -302,9 +309,7 @@
             buf[:, 2 * j + b] = v[VID * b : VID * (b + 1)]
 
     def rows_of(j, k):
-        if k < 2 * FIRST:
-            return u_ref[k, j]
-        return v_ref[k - 2 * FIRST, j] if k < 2 * SPLIT else a_ref[k - 2 * SPLIT, j]
+        return u_ref[k, j]
 
     def inner(j):
         rows = []
@@ -356,17 +361,15 @@
         sends(g).wait()
 
 
-def lower(pos, row_ramp, col_ramp, d, w, gain, u, v, fl, fr, top, low):
+def lower(pos, row_ramp, col_ramp, u, fl, fr, top, low):
     out = jax.ShapeDtypeStruct((VID, 2 * (TC - 2), 16, 2 * U), BF)
-    n = TR - 2 - SPLIT
     return call(
         lower_body,
         "lower",
         out,
-        (pos, row_ramp, col_ramp, d, w, gain, u, v, fl, fr, top, low),
-        2 * n * 416 * 24 * 65536,
+        (pos, row_ramp, col_ramp, u, fl, fr, top, low),
+        1 << 20,
         scratch=[
-            pltpu.VMEM((2 * n, TC - 2, 2 * VID, 2 * U), BF),
             pltpu.VMEM((VID, 2 * (TC - 2), 16, 2 * U), BF),
             pltpu.SemaphoreType.DMA(((TC - 2) // GROUP,)),
         ],
@@ -398,16 +401,15 @@
     gain = norm_gain.reshape(1, U)
     pos = jnp.stack([row_pos, col_pos]).astype(jnp.int32)
     w = fold(ut)
-    d = mix(pos, tok, before, after, cache, entry_weight, cm, wt)
-    left, right = sides(d, w, gain)
+    x, we, dl, dr, left, right = edge(pos, tok, before, after, cache, entry_weight, cm, wt, w, gain)
     from_left = shift(right, "cols", 1)
     from_right = shift(left, "cols", -1)
-    u = upper(d, w, gain, 0, FIRST)
-    top, low = strips(d, w, gain, from_left, from_right, u)
+    d = rest(x, we, cm, wt, dl, dr)
+    top, low = join(*strips(d, w, gain), from_left, from_right)
     from_above = shift(low, "rows", 1)
     from_below = shift(top, "rows", -1)
-    v = upper(d, w, gain, FIRST, SPLIT)
-    out = lower(pos, row_ramp, col_ramp, d, w, gain, u, v, from_left, from_right, from_above, from_below)
+    u = upper(d, w, gain, top)
+    out = lower(pos, row_ramp, col_ramp, u, from_left, from_right, from_above, from_below)
     return jnp.transpose(out, (0, 2, 1, 3))
 
 

time: 66.3 us -> 57.6 us (0.87)
  the two profiles are of different devices: /device:TPU:25 before, /device:TPU:38 now
where the time goes in v1:
time: 57.6 us; the launch traced here: 57.3 us
  Pallas kernels  29.4 us (51%)
  starting transfers between devices  20.5 us (36%)
  local copies, waits for them, and re-layouts  4.42 us (8%)
  waiting for transfers between devices  2.46 us (4%)
    pallas_call x7, Pallas kernels, call(): pl.pallas_call(body, in_specs=specs, out_specs=jax.tree.map(lambda _: VM,...  29.4 us
    ppermute x6, starting transfers between devices, shift(): return lax.ppermute(value, axis, pairs)  20.5 us
    transpose x1, local copies, waits for them, and re-layouts, per_device(): jnp.transpose(cache_middle, (2, 3, 0, 1, 4)).reshape(TR * TC * VID, 2 * C)  3.3 us
    ppermute x6, waiting for transfers between devices, shift(): return lax.ppermute(value, axis, pairs)  2.46 us
  transfers between devices with their start and end apart: 6, of which 1 were waited for; matrix products, arithmetic and copies ran while one was open for 6% of the time, Pallas kernels for 37%

profile of v1, /device:TPU:38, one launch (start us, length us, event | category | flops | bytes accessed | tf_op | source)
XLA Modules:
  0.0 57.3 jit_solution(14435233197042301386)
XLA Ops:
  0.0 1.1 %fusion = (bf16[8,64,52]{2,1,0:T(8,128)(2,1)S(1)}, bf16[8,64,52]{2,1,0:T(8,128)(2,1)S(1)}) fusion(bf16[8,64,208]{2,1,0:T(8,128)(2,1)} %bitcast.13), kind=kLoop, calls=%fused_computation.1 | loop fusion | bytes 212992 | tf_op jit(solution)/shard_map/slice | solution.py:396
  1.1 4.6 %collective-permute-start.1 = (bf16[8,64,52]{2,1,0:T(8,128)(2,1)S(1)}, bf16[8,64,52]{2,1,0:T(8,128)(2,1)S(1)}, u32[]{:S(2)}, u32[]{:S(2)}) collective-permute-start(bf16[8,64,52]{2,1,0:T(8,128)(2,1)S(1)} %get-tuple-element.25), channel_id=1, source_target_pairs={{4,0},{8,4},{12,8},{16,12},{20,16},{24,20},{28,24},{32,28},{36,32}... | collective-permute-start | bytes 159752 | tf_op jit(solution)/shard_map/ppermute | solution.py:22
  5.7 1.9 %collective-permute-start = (bf16[8,64,52]{2,1,0:T(8,128)(2,1)S(1)}, bf16[8,64,52]{2,1,0:T(8,128)(2,1)S(1)}, u32[]{:S(2)}, u32[]{:S(2)}) collective-permute-start(bf16[8,64,52]{2,1,0:T(8,128)(2,1)S(1)} %get-tuple-element.26), channel_id=1, source_target_pairs={{0,4},{4,8},{8,12},{12,16},{16,20},{20,24},{24,28},{28,32},{32,36}... | collective-permute-start | bytes 159752 | tf_op jit(solution)/shard_map/ppermute | solution.py:22
  7.6 0.1 pad_add_fusion.pos_ref
  7.7 0.0 copy-start
  7.7 3.3 %copy.10 = bf16[10,28,8,2,384]{4,2,3,1,0:T(8,128)(2,1)S(1)} copy(bf16[10,28,8,2,384]{4,3,1,0,2:T(2,128)(2,1)} %bitcast.21) | data formatting | bytes 6881280 | tf_op jit(solution)/shard_map/transpose | solution.py:398
  11.0 0.0 copy-start.1
  11.0 0.0 copy-start.4
  11.1 0.0 copy-start.5
  11.1 0.0 copy-start.6
  11.1 0.0 copy-start.7
  11.1 0.0 copy-done
  11.1 0.6 fold.1.w_ref
  11.7 0.0 collective-permute-done.1.after_ref
  11.7 2.4 %collective-permute-done.before_ref = bf16[8,64,52]{2,1,0:T(8,128)(2,1)S(1)} collective-permute-done((bf16[8,64,52]{2,1,0:T(8,128)(2,1)S(1)}, bf16[8,64,52]{2,1,0:T(8,128)(2,1)S(1)}, u32[]{:S(2)}, u32[]{:S(2)}) %collective-permute-start) | collective-permute-done | bytes 53280 | tf_op jit(solution)/shard_map/ppermute | solution.py:22
  14.1 0.0 copy-done.1
  14.1 0.0 copy-done.4
  14.1 0.0 copy-done.5
  14.1 0.0 copy-done.6
  14.1 0.0 copy-done.7
  14.1 4.5 %edge.1 = (bf16[2880,128]{1,0:T(8,128)(2,1)S(1)}, bf16[144,1152]{1,0:T(8,128)(2,1)S(1)}, bf16[12,3,16,384]{3,2,1,0:T(8,128)(2,1)S(1)}, bf16[12,3,16,384]{3,2,1,0...) custom-call(s32[2]{0:T(128)S(1)} %pad_add_fusion.pos_ref, ...), custom_call_target="tpu_custom_call" | custom-call | flops 5242880000 | bytes 65536 | tf_op jit(solution)/shard_map/edge/pallas_call | solution.py:36
  18.7 3.8 %collective-permute-start.2 = (bf16[10,2,16,384]{3,2,1,0:T(8,128)(2,1)S(1)}, bf16[10,2,16,384]{3,2,1,0:T(8,128)(2,1)S(1)}, u32[]{:S(2)}, u32[]{:S(2)}) collective-permute-start(bf16[10,2,16,384]{3,2,1,0:T(8,128)(2,1)S(1)} %get-tuple-element.21), channel_id=1, source_target_pairs={{0,1},{1,2},{2,3},{4,5},{5,6},{6,7},{8,9},{9,10},{10,11},{12,13},{... | collective-permute-start | bytes 737288 | tf_op jit(solution)/shard_map/ppermute | solution.py:22
  22.5 2.2 %collective-permute-start.3 = (bf16[10,2,16,384]{3,2,1,0:T(8,128)(2,1)S(1)}, bf16[10,2,16,384]{3,2,1,0:T(8,128)(2,1)S(1)}, u32[]{:S(2)}, u32[]{:S(2)}) collective-permute-start(bf16[10,2,16,384]{3,2,1,0:T(8,128)(2,1)S(1)} %get-tuple-element.22), channel_id=1, source_target_pairs={{1,0},{2,1},{3,2},{5,4},{6,5},{7,6},{9,8},{10,9},{11,10},{13,12},{... | collective-permute-start | bytes 737288 | tf_op jit(solution)/shard_map/ppermute | solution.py:22
  24.7 5.8 %rest.1.d_ref = bf16[12,30,16,384]{3,2,1,0:T(8,128)(2,1)S(1)} custom-call(bf16[2880,128]{1,0:T(8,128)(2,1)S(1)} %get-tuple-element.15.x_ref, bf16[144,1152]{1,0:T(8,128)(2,1)S(1)} %get-tuple-element.16.we_ref, bf16[2240,768]{1,0:T(8,128)(2,1)S(1)} %bitcast.11, bf16[1152,768]{1,0:T(8,128)(2,1)S(1)} %bitcast.16, ...), custom_call_target="tpu_custom_call" | custom-call | flops 5898240000 | bytes 65536 | tf_op jit(solution)/shard_map/rest/pallas_call | solution.py:36
  30.6 3.6 %strips.1 = (bf16[2,26,16,384]{3,2,1,0:T(8,128)(2,1)S(1)}, bf16[2,26,16,384]{3,2,1,0:T(8,128)(2,1)S(1)}) custom-call(bf16[12,30,16,384]{3,2,1,0:T(8,128)(2,1)S(1)} %rest.1.d_ref, bf16[4,256,1536]{2,1,0:T(8,128)(2,1)S(1)} %fold.1.w_ref, f32[1,192]{1,0:T(1,128)S(1)} %bitcast.19), custom_call_target="tpu_custom_call" | custom-call | flops 2617245696 | bytes 65536 | tf_op jit(solution)/shard_map/strips/pallas_call | solution.py:36
  34.2 0.0 collective-permute-done.2.fl_ref
  34.2 0.0 collective-permute-done.3.fr_ref
  34.2 0.1 join.1
  34.3 1.9 %collective-permute-start.4 = (bf16[2,28,16,384]{3,2,1,0:T(8,128)(2,1)S(1)}, bf16[2,28,16,384]{3,2,1,0:T(8,128)(2,1)S(1)}, u32[]{:S(2)}, u32[]{:S(2)}) collective-permute-start(bf16[2,28,16,384]{3,2,1,0:T(8,128)(2,1)S(1)} %get-tuple-element.24), channel_id=1, source_target_pairs={{0,4},{4,8},{8,12},{12,16},{16,20},{20,24},{24,28},{28,32},{32,36}... | collective-permute-start | bytes 2064392 | tf_op jit(solution)/shard_map/ppermute | solution.py:22
  36.3 0.0 copy-start.2
  36.3 0.0 copy-start.3
  36.3 6.0 %collective-permute-start.5 = (bf16[2,28,16,384]{3,2,1,0:T(8,128)(2,1)S(1)}, bf16[2,28,16,384]{3,2,1,0:T(8,128)(2,1)S(1)}, u32[]{:S(2)}, u32[]{:S(2)}) collective-permute-start(bf16[2,28,16,384]{3,2,1,0:T(8,128)(2,1)S(1)} %get-tuple-element.23.after_ref), channel_id=1, source_target_pairs={{4,0},{8,4},{12,8},{16,12},{20,16},{24,20},{28,24},{32,28},{36,32}... | collective-permute-start | bytes 2064392 | tf_op jit(solution)/shard_map/ppermute | solution.py:22
  42.3 11.2 %upper.1.u_ref = bf16[16,26,16,384]{3,2,1,0:T(8,128)(2,1)S(1)} custom-call(bf16[12,30,16,384]{3,2,1,0:T(8,128)(2,1)S(1)} %rest.1.d_ref, bf16[4,256,1536]{2,1,0:T(8,128)(2,1)S(1)} %fold.1.w_ref, f32[1,192]{1,0:T(1,128)S(1)} %bitcast.20, bf16[2,28,16,384]{3,2,1,0:T(8,128)(2,1)S(1)} %get-tuple-element.23.after_ref), custom_call_target="tpu_custom_call" | custom-call | flops 10468982784 | bytes 65536 | tf_op jit(solution)/shard_map/upper/pallas_call | solution.py:36
  53.5 0.0 collective-permute-done.4.top_ref
  53.5 0.0 collective-permute-done.5.low_ref
  53.5 0.0 copy-done.2
  53.5 0.0 copy-done.3
  53.5 3.6 %lower.1 = bf16[8,52,16,384]{3,2,1,0:T(8,128)(2,1)} custom-call(s32[2]{0:T(128)S(1)} %pad_add_fusion.pos_ref, s32[32]{0:T(128)S(1)} %copy-done.2, s32[4]{0:T(128)S(1)} %copy-done.3, bf16[16,26,16,384]{3,2,1,0:T(8,128)(2,1)S(1)} %upper.1.u_ref, bf16[10,2,16,384]{3,2,1,0:T(8,128)(2,1)S(1)} %collective-permute-done.2.fl_ref, ...), custom_call_target="tpu_custom_call" | custom-call | flops 1048576 | bytes 65536 | tf_op jit(solution)/shard_map/lower/pallas_call | solution.py:36
Async XLA Ops:
  1.1 10.6 %collective-permute-start.1 = (bf16[8,64,52]{2,1,0:T(8,128)(2,1)S(1)}, bf16[8,64,52]{2,1,0:T(8,128)(2,1)S(1)}, u32[]{:S(2)}, u32[]{:S(2)}) collective-permute-start(bf16[8,64,52]{2,1,0:T(8,128)(2,1)S(1)} %get-tuple-element.25), channel_id=1, source_target_pairs={{4,0},{8,4},{12,8},{16,12},{20,16},{24,20},{28,24},{32,28},{36,32}... | collective-permute-start | bytes 159752 | tf_op jit(solution)/shard_map/ppermute | solution.py:22
  5.7 8.4 %collective-permute-start = (bf16[8,64,52]{2,1,0:T(8,128)(2,1)S(1)}, bf16[8,64,52]{2,1,0:T(8,128)(2,1)S(1)}, u32[]{:S(2)}, u32[]{:S(2)}) collective-permute-start(bf16[8,64,52]{2,1,0:T(8,128)(2,1)S(1)} %get-tuple-element.26), channel_id=1, source_target_pairs={{0,4},{4,8},{8,12},{12,16},{16,20},{20,24},{24,28},{28,32},{32,36}... | collective-permute-start | bytes 159752 | tf_op jit(solution)/shard_map/ppermute | solution.py:22
  7.7 3.4 %copy-start = (bf16[3,3,384,192]{2,3,1,0:T(8,128)(2,1)S(1)}, bf16[3,3,384,192]{2,3,1,0:T(8,128)(2,1)}, u32[]{:S(2)}) copy-start(bf16[3,3,384,192]{2,3,1,0:T(8,128)(2,1)} %param.14) | copy-start | bytes 3981316
  11.0 3.1 %copy-start.1 = (bf16[8,208,64]{1,2,0:T(8,128)(2,1)S(1)}, bf16[8,208,64]{1,2,0:T(8,128)(2,1)}, u32[]{:S(2)}) copy-start(bf16[8,208,64]{1,2,0:T(8,128)(2,1)} %param.9) | copy-start | bytes 638980
  11.0 3.1 %copy-start.4 = (bf16[3,384,768]{2,1,0:T(8,128)(2,1)S(1)}, bf16[3,384,768]{2,1,0:T(8,128)(2,1)}, u32[]{:S(2)}) copy-start(bf16[3,384,768]{2,1,0:T(8,128)(2,1)} %param.13) | copy-start | bytes 5308420
  11.1 3.1 %copy-start.5 = (bf16[8,2,10,28,16]{3,4,2,1,0:T(8,128)(2,1)S(1)}, bf16[8,2,10,28,16]{3,4,2,1,0:T(8,128)(2,1)}, u32[]{:S(2)}) copy-start(bf16[8,2,10,28,16]{3,4,2,1,0:T(8,128)(2,1)} %param.10) | copy-start | bytes 430084
  11.1 3.1 %copy-start.6 = (bf16[3,3,3,16,384]{4,3,2,1,0:T(8,128)(2,1)S(1)}, bf16[3,3,3,16,384]{4,3,2,1,0:T(8,128)(2,1)}, u32[]{:S(2)}) copy-start(bf16[3,3,3,16,384]{4,3,2,1,0:T(8,128)(2,1)} %ew_ref.1) | copy-start | bytes 995332
  11.1 3.1 %copy-start.7 = (f32[192]{0:T(256)S(1)}, f32[192]{0:T(256)}, u32[]{:S(2)}) copy-start(f32[192]{0:T(256)} %param.15) | copy-start | bytes 2308
  18.7 15.5 %collective-permute-start.2 = (bf16[10,2,16,384]{3,2,1,0:T(8,128)(2,1)S(1)}, bf16[10,2,16,384]{3,2,1,0:T(8,128)(2,1)S(1)}, u32[]{:S(2)}, u32[]{:S(2)}) collective-permute-start(bf16[10,2,16,384]{3,2,1,0:T(8,128)(2,1)S(1)} %get-tuple-element.21), channel_id=1, source_target_pairs={{0,1},{1,2},{2,3},{4,5},{5,6},{6,7},{8,9},{9,10},{10,11},{12,13},{... | collective-permute-start | bytes 737288 | tf_op jit(solution)/shard_map/ppermute | solution.py:22
  22.5 11.7 %collective-permute-start.3 = (bf16[10,2,16,384]{3,2,1,0:T(8,128)(2,1)S(1)}, bf16[10,2,16,384]{3,2,1,0:T(8,128)(2,1)S(1)}, u32[]{:S(2)}, u32[]{:S(2)}) collective-permute-start(bf16[10,2,16,384]{3,2,1,0:T(8,128)(2,1)S(1)} %get-tuple-element.22), channel_id=1, source_target_pairs={{1,0},{2,1},{3,2},{5,4},{6,5},{7,6},{9,8},{10,9},{11,10},{13,12},{... | collective-permute-start | bytes 737288 | tf_op jit(solution)/shard_map/ppermute | solution.py:22
  34.3 19.1 %collective-permute-start.4 = (bf16[2,28,16,384]{3,2,1,0:T(8,128)(2,1)S(1)}, bf16[2,28,16,384]{3,2,1,0:T(8,128)(2,1)S(1)}, u32[]{:S(2)}, u32[]{:S(2)}) collective-permute-start(bf16[2,28,16,384]{3,2,1,0:T(8,128)(2,1)S(1)} %get-tuple-element.24), channel_id=1, source_target_pairs={{0,4},{4,8},{8,12},{12,16},{16,20},{20,24},{24,28},{28,32},{32,36}... | collective-permute-start | bytes 2064392 | tf_op jit(solution)/shard_map/ppermute | solution.py:22
  36.3 17.2 %copy-start.2 = (s32[32]{0:T(128)S(1)}, s32[32]{0:T(128)}, u32[]{:S(2)}) copy-start(s32[32]{0:T(128)} %rr_ref.1) | copy-start | bytes 388
  36.3 17.2 %copy-start.3 = (s32[4]{0:T(128)S(1)}, s32[4]{0:T(128)}, u32[]{:S(2)}) copy-start(s32[4]{0:T(128)} %cr_ref.1) | copy-start | bytes 52
  36.3 17.2 %collective-permute-start.5 = (bf16[2,28,16,384]{3,2,1,0:T(8,128)(2,1)S(1)}, bf16[2,28,16,384]{3,2,1,0:T(8,128)(2,1)S(1)}, u32[]{:S(2)}, u32[]{:S(2)}) collective-permute-start(bf16[2,28,16,384]{3,2,1,0:T(8,128)(2,1)S(1)} %get-tuple-element.23.after_ref), channel_id=1, source_target_pairs={{4,0},{8,4},{12,8},{16,12},{20,16},{24,20},{28,24},{32,28},{36,32}... | collective-permute-start | bytes 2064392 | tf_op jit(solution)/shard_map/ppermute | solution.py:22

commit v2 on v1

--- a/solution.py
+++ b/solution.py
@@ -20,6 +20,12 @@
     size = lax.axis_size(axis)
     pairs = [(i, i + step) for i in range(size) if 0 <= i + step < size]
     return lax.ppermute(value, axis, pairs)
+
+
+def swap(value, first):
+    size = lax.axis_size("rows")
+    pairs = [(i, i + 1) for i in range(first, size - 1, 2)]
+    return lax.ppermute(value, "rows", pairs + [(j, i) for i, j in pairs])
 
 
 VM = pl.BlockSpec(memory_space=pltpu.VMEM)
@@ -125,6 +131,8 @@
     t_ref,
     lat_ref,
     old_ref,
+    sl_ref,
+    sr_ref,
 ):
     dl_ref[...] = jnp.zeros(dl_ref.shape, BF)
     dr_ref[...] = jnp.zeros(dr_ref.shape, BF)
@@ -137,9 +145,11 @@
     d = mixed(x_ref, we_ref, cm_ref, wt_ref, ((0, TR, 0, 2), (0, TR, TC - 2, 2)))
     dl_ref[1 : TR + 1, 1:3] = d[: 2 * TR].reshape(TR, 2, 2 * VID, C)
     dr_ref[1 : TR + 1, 0:2] = d[2 * TR :].reshape(TR, 2, 2 * VID, C)
+    sl_ref[...] = steps_right(dl_ref[...])
+    sr_ref[...] = steps_right(dr_ref[...])
     gain = half_gain(gain_ref)
     for a in range(2):
-        v = both(w_ref, gain, ((dl_ref, 0, TR, 0, 1), (dr_ref, 0, TR, 0, 1)), a)
+        v = both(w_ref, gain, ((dl_ref, sl_ref, 0, TR, 0, 1), (dr_ref, sr_ref, 0, TR, 0, 1)), a)
         left_ref[:, a] = v[:TR]
         right_ref[:, a] = v[TR:]
 
@@ -158,61 +168,57 @@
             pltpu.VMEM((2, 6 * PITCH + 8, 128), F32),
             pltpu.VMEM((12 * WIDE, 128), F32),
             pltpu.VMEM((12 * WIDE, 128), F32),
+            pltpu.VMEM((TR + 2, 2, 2 * VID, C), BF),
+            pltpu.VMEM((TR + 2, 2, 2 * VID, C), BF),
         ],
         smem=1,
     )
 
 
-def rest_body(x_ref, we_ref, cm_ref, wt_ref, dl_ref, dr_ref, d_ref):
+def rest_body(x_ref, we_ref, cm_ref, wt_ref, dl_ref, dr_ref, d_ref, s_ref):
     n = TC - 4
     line = jnp.zeros((1, n, 2 * VID, C), BF)
     d_ref[0:1, 3 : n + 3] = line
     d_ref[TR + 1 : TR + 2, 3 : n + 3] = line
     d_ref[:, 0:3] = dl_ref[...]
     d_ref[:, n + 3 : n + 6] = dr_ref[...]
+    for i in (0, TR + 1):
+        s_ref[i] = jnp.zeros((TC + 1, 2 * VID, C), BF)
     rows = TR // STEPS
     for g in range(STEPS):
         d = mixed(x_ref, we_ref, cm_ref, wt_ref, ((g * rows, rows, 2, n),))
         d_ref[1 + g * rows : 1 + (g + 1) * rows, 3 : n + 3] = d.reshape(rows, n, 2 * VID, C)
+        for i in range(1 + g * rows, 1 + (g + 1) * rows):
+            s_ref[i : i + 1] = steps_right(d_ref[i : i + 1])
 
 
 def rest(x, we, cm, wt, dl, dr):
-    out = pltpu.VMEM((TR + 2, TC + 2, 2 * VID, C), BF)
-    return call(rest_body, "rest", out, (x, we, cm, wt, dl, dr), 2 * 45000 * 65536)
+    outs = (pltpu.VMEM((TR + 2, TC + 2, 2 * VID, C), BF), pltpu.VMEM((TR + 2, TC + 1, 2 * VID, C), BF))
+    return call(rest_body, "rest", outs, (x, we, cm, wt, dl, dr), 2 * 45000 * 65536)
 
 
 def fold_body(ut_ref, w_ref):
-    def sums(get):
-        return (get(0), get(1) + get(2)), (get(0) + get(1), get(2))
-
-    rows = [sums(lambda r: ut_ref[r, c].astype(F32)) for c in range(3)]
     for a in range(2):
         for kr in range(2):
-            cols = sums(lambda c: rows[c][a][kr])
-            for b in range(2):
-                for kc in range(2):
-                    w = cols[b][kc].astype(BF)
-                    at = (kr * 2 + kc) * C
-                    w_ref[2 * a + b, 0:U, at : at + C] = w
-                    w_ref[2 * a + b, U:256, at : at + C] = w[0:64]
+            rows = (((0,), (1, 2)), ((0, 1), (2,)))[a][kr]
+            cols = [functools.reduce(jnp.add, [ut_ref[r, c].astype(F32) for r in rows]) for c in range(3)]
+            for k, w in enumerate((cols[0] + cols[1] + cols[2], -cols[0], cols[2])):
+                w = w.astype(BF)
+                w_ref[a, k, 0:U, kr * C : (kr + 1) * C] = w
+                w_ref[a, k, U:256, kr * C : (kr + 1) * C] = w[0:64]
 
 
 def fold(ut):
-    return call(fold_body, "fold", pltpu.VMEM((4, 256, 4 * C), BF), (ut,), 1 << 24)
-
-
-def phase(w_ref, gain, areas, a, b):
-    parts, cells = [], 0
-    for d_ref, i0, ni, j0, nj in areas:
-        taps = [
-            d_ref[i0 + a + kr : i0 + a + kr + ni, j0 + b + kc : j0 + b + kc + nj].reshape(ni * nj * 2 * VID, C)
-            for kr in range(2)
-            for kc in range(2)
-        ]
-        parts.append(jnp.concatenate(taps, axis=1))
-        cells += ni * nj
-    full = jnp.concatenate(parts, axis=0) if len(parts) > 1 else parts[0]
-    res = lax.dot_general(full, w_ref[2 * a + b], NT, preferred_element_type=F32)
+    return call(fold_body, "fold", pltpu.VMEM((2, 3, 256, 2 * C), BF), (ut,), 1 << 24)
+
+
+def steps_right(value):
+    n = value.shape[1]
+    return (value[:, 1:].astype(F32) - value[:, : n - 1].astype(F32)).astype(BF)
+
+
+def activate(res, gain):
+    cells = res.shape[0] // (2 * VID)
     res = res.reshape(cells, 2, VID, 256)
     one = res[:, 0].reshape(cells * VID, 256)
     two = res[:, 1].reshape(cells * VID, 256)
@@ -225,63 +231,96 @@
     s1 = jnp.sum(o2 * o2 + jnp.where(low, 0.0, q1), axis=1, keepdims=True)
     r0 = lax.rsqrt(s0 * (1.0 / U) + EPSILON)
     r1 = lax.rsqrt(s1 * (1.0 / U) + EPSILON)
-    o2 = pltpu.roll(o2, 64, 1)
     outs = []
     for k, (o, r) in enumerate(((o0, r0), (o1, jnp.where(low, r0, r1)), (o2, r1))):
         h = o * r * gain[:, 128 * k : 128 * (k + 1)]
-        outs.append(h + h * jnp.tanh(h))
-    return jnp.concatenate(outs, axis=1)
+        outs.append((h + h * jnp.tanh(h)).reshape(cells, 1, VID, 128))
+    return outs
 
 
 def both(w_ref, gain, areas, a):
-    n = sum(area[2] * area[4] for area in areas)
-    outs = [phase(w_ref, gain, areas, a, b).reshape(n, 1, VID, 2 * U) for b in range(2)]
-    return jnp.concatenate(outs, axis=1).reshape(n, 2 * VID, 2 * U).astype(BF)
+    def pick(which, shift):
+        parts = []
+        for area in areas:
+            ref, (i0, ni, j0, nj) = area[which], area[2:]
+            taps = [
+                ref[i0 + a + kr : i0 + a + kr + ni, j0 + shift : j0 + shift + nj].reshape(ni * nj * 2 * VID, C)
+                for kr in range(2)
+            ]
+            parts.append(jnp.concatenate(taps, axis=1))
+        return jnp.concatenate(parts, axis=0) if len(parts) > 1 else parts[0]
+
+    def times(lhs, k):
+        return lax.dot_general(lhs, w_ref[a, k], NT, preferred_element_type=F32)
+
+    n = sum(area[3] * area[5] for area in areas)
+    shared = times(pick(0, 1), 0)
+    sides = [activate(shared + times(pick(1, b), 1 + b), gain) for b in range(2)]
+    outs = [jnp.concatenate([u, v], axis=1).reshape(n, 2 * VID, 128).astype(BF) for u, v in zip(*sides)]
+    outs[2] = jnp.concatenate([outs[2][:, :, 64:], outs[2][:, :, :64]], axis=2)
+    return jnp.concatenate(outs, axis=2)
 
 
 def half_gain(gain_ref):
-    return jnp.concatenate([gain_ref[...], gain_ref[...]], axis=1) * 0.5
-
-
-def strips_body(d_ref, w_ref, gain_ref, top_ref, low_ref):
+    g = gain_ref[...] * 0.5
+    return jnp.concatenate([g, g[:, :64], g[:, 128:], g[:, 64:128]], axis=1)
+
+
+def strips_body(d_ref, s_ref, w_ref, gain_ref, top_ref, low_ref):
     gain = half_gain(gain_ref)
     n = TC - 2
     for a in range(2):
-        v = both(w_ref, gain, ((d_ref, 0, 1, 1, n), (d_ref, TR - 1, 1, 1, n)), a)
-        top_ref[a] = v[:n]
-        low_ref[a] = v[n:]
-
-
-def strips(d, w, gain):
+        for i, ref in ((0, top_ref), (TR - 1, low_ref)):
+            ref[a] = both(w_ref, gain, ((d_ref, s_ref, i, 1, 1, n),), a)
+
+
+def strips(d, s, w, gain):
     strip = pltpu.VMEM((2, TC - 2, 2 * VID, 2 * U), BF)
-    return call(strips_body, "strips", (strip, strip), (d, w, gain), 2 * 832 * 24 * 65536)
-
-
-def join_body(t_ref, l_ref, fl_ref, fr_ref, top_ref, low_ref):
+    return call(strips_body, "strips", (strip, strip), (d, s, w, gain), 2 * 832 * 18 * 65536)
+
+
+def join_body(pos_ref, t_ref, l_ref, fl_ref, fr_ref, even_ref, odd_ref):
     n = TC - 2
-    for ref, own_ref, i in ((top_ref, t_ref, 0), (low_ref, l_ref, TR - 1)):
+    even = pos_ref[0] % 2 == 0
+
+    def put(ref, own_ref, i):
         ref[:, 1 : n + 1] = own_ref[...]
         for a in range(2):
             ref[a, 0] = fl_ref[i, a]
             ref[a, n + 1] = fr_ref[i, a]
 
-
-def join(t, l, fl, fr):
+    @pl.when(even)
+    def _():
+        put(even_ref, l_ref, TR - 1)
+        put(odd_ref, t_ref, 0)
+
+    @pl.when(jnp.logical_not(even))
+    def _():
+        put(even_ref, t_ref, 0)
+        put(odd_ref, l_ref, TR - 1)
+
+
+def join(pos, t, l, fl, fr):
     strip = jax.ShapeDtypeStruct((2, TC, 2 * VID, 2 * U), BF)
-    return call(join_body, "join", (strip, strip), (t, l, fl, fr), 1 << 20)
-
-
-def upper_body(d_ref, w_ref, gain_ref, after_ref, o_ref):
+    return call(join_body, "join", (strip, strip), (pos, t, l, fl, fr), 1 << 20, smem=1)
+
+
+CHUNK = 26
+
+
+def upper_body(d_ref, s_ref, w_ref, gain_ref, after_ref, o_ref):
     del after_ref
     gain = half_gain(gain_ref)
     for i in range(TR - 2):
         for a in range(2):
-            o_ref[2 * i + a] = both(w_ref, gain, ((d_ref, i + 1, 1, 1, TC - 2),), a)
-
-
-def upper(d, w, gain, after):
+            for j in range(0, TC - 2, CHUNK):
+                area = (d_ref, s_ref, i + 1, 1, 1 + j, CHUNK)
+                o_ref[2 * i + a, j : j + CHUNK] = both(w_ref, gain, (area,), a)
+
+
+def upper(d, s, w, gain, after):
     out = pltpu.VMEM((2 * (TR - 2), TC - 2, 2 * VID, 2 * U), BF)
-    return call(upper_body, "upper", out, (d, w, gain, after), 2 * (TR - 2) * 416 * 24 * 65536)
+    return call(upper_body, "upper", out, (d, s, w, gain, after), 2 * (TR - 2) * 416 * 18 * 65536)
 
 
 def ramp(pos, table_ref, amount, place):
@@ -293,11 +332,18 @@
 GROUP = 2
 
 
-def lower_body(pos_ref, rr_ref, cr_ref, u_ref, fl_ref, fr_ref, top_ref, low_ref, o_ref, buf, sem):
+def lower_body(pos_ref, rr_ref, cr_ref, u_ref, fl_ref, fr_ref, even_ref, odd_ref, o_ref, buf, sem):
     r, c = pos_ref[0], pos_ref[1]
     up = [ramp(r, rr_ref, ROWS, p) for p in (0, 1)]
     down = [ramp(r + 1, rr_ref, ROWS, p) for p in (-2, -1)]
     groups = (TC - 2) // GROUP
+    even = jnp.full((2 * VID, 1), r % 2, jnp.int32) == 0
+
+    def above(p, j):
+        return jnp.where(even, odd_ref[p, j].astype(F32), even_ref[p, j].astype(F32))
+
+    def below(p, j):
+        return jnp.where(even, even_ref[p, j].astype(F32), odd_ref[p, j].astype(F32))
 
     def sends(g):
         at = pl.ds(g * 2 * GROUP, 2 * GROUP)
@@ -316,10 +362,10 @@
         for p in range(16):
             v = rows_of(j, p)
             if p < 2:
-                v = (v.astype(F32) * up[p] + top_ref[p, j + 1].astype(F32) * (1.0 - up[p])).astype(BF)
+                v = (v.astype(F32) * up[p] + above(p, j + 1) * (1.0 - up[p])).astype(BF)
             elif p > 13:
                 w = down[p - 14]
-                v = (v.astype(F32) * (1.0 - w) + low_ref[p - 14, j + 1].astype(F32) * w).astype(BF)
+                v = (v.astype(F32) * (1.0 - w) + below(p - 14, j + 1) * w).astype(BF)
             rows.append(v[None])
         put(j, jnp.concatenate(rows, axis=0))
 
@@ -334,10 +380,10 @@
         for p in range(16):
             v = across(rows_of(j, p), side_ref[1 + p // 2, p % 2])
             if p < 2:
-                v = v * up[p] + across(top_ref[p, j + 1], top_ref[p, slot]) * (1.0 - up[p])
+                v = v * up[p] + across(above(p, j + 1), above(p, slot)) * (1.0 - up[p])
             elif p > 13:
                 k = down[p - 14]
-                v = v * (1.0 - k) + across(low_ref[p - 14, j + 1], low_ref[p - 14, slot]) * k
+                v = v * (1.0 - k) + across(below(p - 14, j + 1), below(p - 14, slot)) * k
             rows.append(v.astype(BF)[None])
         put(j, jnp.concatenate(rows, axis=0))
 
@@ -361,13 +407,13 @@
         sends(g).wait()
 
 
-def lower(pos, row_ramp, col_ramp, u, fl, fr, top, low):
+def lower(pos, row_ramp, col_ramp, u, fl, fr, even, odd):
     out = jax.ShapeDtypeStruct((VID, 2 * (TC - 2), 16, 2 * U), BF)
     return call(
         lower_body,
         "lower",
         out,
-        (pos, row_ramp, col_ramp, u, fl, fr, top, low),
+        (pos, row_ramp, col_ramp, u, fl, fr, even, odd),
         1 << 20,
         scratch=[
             pltpu.VMEM((VID, 2 * (TC - 2), 16, 2 * U), BF),
@@ -404,12 +450,12 @@
     x, we, dl, dr, left, right = edge(pos, tok, before, after, cache, entry_weight, cm, wt, w, gain)
     from_left = shift(right, "cols", 1)
     from_right = shift(left, "cols", -1)
-    d = rest(x, we, cm, wt, dl, dr)
-    top, low = join(*strips(d, w, gain), from_left, from_right)
-    from_above = shift(low, "rows", 1)
-    from_below = shift(top, "rows", -1)
-    u = upper(d, w, gain, top)
-    out = lower(pos, row_ramp, col_ramp, u, from_left, from_right, from_above, from_below)
+    d, s = rest(x, we, cm, wt, dl, dr)
+    to_even, to_odd = join(pos, *strips(d, s, w, gain), from_left, from_right)
+    by_odd = swap(to_odd, 1)
+    by_even = swap(to_even, 0)
+    u = upper(d, s, w, gain, to_even)
+    out = lower(pos, row_ramp, col_ramp, u, from_left, from_right, by_even, by_odd)
     return jnp.transpose(out, (0, 2, 1, 3))
 
 

time: 57.6 us -> 52.7 us (0.915)
  starting transfers between devices: 20.5 us -> 17 us
  Pallas kernels: 29.4 us -> 27.1 us
  waiting for transfers between devices: 2.46 us -> 3.49 us
    ppermute x6 -> x4, starting transfers between devices: 20.5 us -> 12.6 us  [shift(): return lax.ppermute(value, axis, pairs)]
    ppermute x0 -> x2, starting transfers between devices: none -> 4.38 us  [swap(): return lax.ppermute(value, 'rows', pairs + [(j, i) for i, j in pairs])]
    pallas_call x7, Pallas kernels: 29.4 us -> 27.1 us  [call(): pl.pallas_call(body, in_specs=specs, out_specs=jax.tree.map(lambda _: VM,...]
    ppermute x0 -> x2, waiting for transfers between devices: none -> 0.95 us  [swap(): return lax.ppermute(value, 'rows', pairs + [(j, i) for i, j in pairs])]
    ppermute x6 -> x4, waiting for transfers between devices: 2.46 us -> 2.54 us  [shift(): return lax.ppermute(value, axis, pairs)]
  transfers between devices with their start and end apart: 6 -> 6, of which waited for: 1 -> 2; matrix products, arithmetic and copies ran while one was open for 6% -> 6% of each run, Pallas kernels for 37% -> 35%
where the time goes in v2:
time: 52.7 us; the launch traced here: 52.4 us
  Pallas kernels  27.1 us (51%)
  starting transfers between devices  17 us (32%)
  local copies, waits for them, and re-layouts  4.42 us (8%)
  waiting for transfers between devices  3.49 us (7%)
    pallas_call x7, Pallas kernels, call(): pl.pallas_call(body, in_specs=specs, out_specs=jax.tree.map(lambda _: VM,...  27.1 us
    ppermute x4, starting transfers between devices, shift(): return lax.ppermute(value, axis, pairs)  12.6 us
    ppermute x2, starting transfers between devices, swap(): return lax.ppermute(value, 'rows', pairs + [(j, i) for i, j in pairs])  4.38 us
    transpose x1, local copies, waits for them, and re-layouts, per_device(): jnp.transpose(cache_middle, (2, 3, 0, 1, 4)).reshape(TR * TC * VID, 2 * C)  3.3 us
    ppermute x4, waiting for transfers between devices, shift(): return lax.ppermute(value, axis, pairs)  2.54 us
    slice x1, local copies, waits for them, and re-layouts, per_device(): after = shift(tok[:, :, :52], 'rows', -1)  1.07 us
  transfers between devices with their start and end apart: 6, of which 2 were waited for; matrix products, arithmetic and copies ran while one was open for 6% of the time, Pallas kernels for 35%

profile of v2, /device:TPU:38, one launch (start us, length us, event | category | flops | bytes accessed | tf_op | source)
XLA Modules:
  0.0 52.4 jit_solution(6811338272721403844)
XLA Ops:
  0.0 1.1 %fusion = (bf16[8,64,52]{2,1,0:T(8,128)(2,1)S(1)}, bf16[8,64,52]{2,1,0:T(8,128)(2,1)S(1)}) fusion(bf16[8,64,208]{2,1,0:T(8,128)(2,1)} %bitcast.13), kind=kLoop, calls=%fused_computation.1 | loop fusion | bytes 212992 | tf_op jit(solution)/shard_map/slice | solution.py:442
  1.1 4.6 %collective-permute-start.1 = (bf16[8,64,52]{2,1,0:T(8,128)(2,1)S(1)}, bf16[8,64,52]{2,1,0:T(8,128)(2,1)S(1)}, u32[]{:S(2)}, u32[]{:S(2)}) collective-permute-start(bf16[8,64,52]{2,1,0:T(8,128)(2,1)S(1)} %get-tuple-element.29), channel_id=1, source_target_pairs={{4,0},{8,4},{12,8},{16,12},{20,16},{24,20},{28,24},{32,28},{36,32}... | collective-permute-start | bytes 159752 | tf_op jit(solution)/shard_map/ppermute | solution.py:22
  5.7 1.9 %collective-permute-start = (bf16[8,64,52]{2,1,0:T(8,128)(2,1)S(1)}, bf16[8,64,52]{2,1,0:T(8,128)(2,1)S(1)}, u32[]{:S(2)}, u32[]{:S(2)}) collective-permute-start(bf16[8,64,52]{2,1,0:T(8,128)(2,1)S(1)} %get-tuple-element.30), channel_id=1, source_target_pairs={{0,4},{4,8},{8,12},{12,16},{16,20},{20,24},{24,28},{28,32},{32,36}... | collective-permute-start | bytes 159752 | tf_op jit(solution)/shard_map/ppermute | solution.py:22
  7.6 0.1 pad_add_fusion.pos_ref
  7.7 0.0 copy-start
  7.7 3.3 %copy.10 = bf16[10,28,8,2,384]{4,2,3,1,0:T(8,128)(2,1)S(1)} copy(bf16[10,28,8,2,384]{4,3,1,0,2:T(2,128)(2,1)} %bitcast.21) | data formatting | bytes 6881280 | tf_op jit(solution)/shard_map/transpose | solution.py:444
  11.0 0.0 copy-start.1
  11.0 0.0 copy-start.2
  11.1 0.0 copy-start.5
  11.1 0.0 copy-start.6
  11.1 0.0 copy-start.7
  11.1 0.0 copy-done
  11.1 0.5 fold.1.w_ref
  11.6 0.0 collective-permute-done.1.after_ref
  11.6 2.5 %collective-permute-done.before_ref = bf16[8,64,52]{2,1,0:T(8,128)(2,1)S(1)} collective-permute-done((bf16[8,64,52]{2,1,0:T(8,128)(2,1)S(1)}, bf16[8,64,52]{2,1,0:T(8,128)(2,1)S(1)}, u32[]{:S(2)}, u32[]{:S(2)}) %collective-permute-start) | collective-permute-done | bytes 53280 | tf_op jit(solution)/shard_map/ppermute | solution.py:22
  14.1 0.0 copy-done.1
  14.1 0.0 copy-done.2
  14.1 0.0 copy-done.5
  14.1 0.0 copy-done.6
  14.1 0.0 copy-done.7
  14.1 4.6 %edge.1 = (bf16[2880,128]{1,0:T(8,128)(2,1)S(1)}, bf16[144,1152]{1,0:T(8,128)(2,1)S(1)}, bf16[12,3,16,384]{3,2,1,0:T(8,128)(2,1)S(1)}, bf16[12,3,16,384]{3,2,1,0...) custom-call(s32[2]{0:T(128)S(1)} %pad_add_fusion.pos_ref, ...), custom_call_target="tpu_custom_call" | custom-call | flops 5242880000 | bytes 65536 | tf_op jit(solution)/shard_map/edge/pallas_call | solution.py:42
  18.7 3.8 %collective-permute-start.2 = (bf16[10,2,16,384]{3,2,1,0:T(8,128)(2,1)S(1)}, bf16[10,2,16,384]{3,2,1,0:T(8,128)(2,1)S(1)}, u32[]{:S(2)}, u32[]{:S(2)}) collective-permute-start(bf16[10,2,16,384]{3,2,1,0:T(8,128)(2,1)S(1)} %get-tuple-element.25), channel_id=1, source_target_pairs={{0,1},{1,2},{2,3},{4,5},{5,6},{6,7},{8,9},{9,10},{10,11},{12,13},{... | collective-permute-start | bytes 737288 | tf_op jit(solution)/shard_map/ppermute | solution.py:22
  22.5 2.2 %collective-permute-start.3 = (bf16[10,2,16,384]{3,2,1,0:T(8,128)(2,1)S(1)}, bf16[10,2,16,384]{3,2,1,0:T(8,128)(2,1)S(1)}, u32[]{:S(2)}, u32[]{:S(2)}) collective-permute-start(bf16[10,2,16,384]{3,2,1,0:T(8,128)(2,1)S(1)} %get-tuple-element.26), channel_id=1, source_target_pairs={{1,0},{2,1},{3,2},{5,4},{6,5},{7,6},{9,8},{10,9},{11,10},{13,12},{... | collective-permute-start | bytes 737288 | tf_op jit(solution)/shard_map/ppermute | solution.py:22
  24.8 6.2 %rest.1 = (bf16[12,30,16,384]{3,2,1,0:T(8,128)(2,1)S(1)}, bf16[12,29,16,384]{3,2,1,0:T(8,128)(2,1)S(1)}) custom-call(bf16[2880,128]{1,0:T(8,128)(2,1)S(1)} %get-tuple-element.17.x_ref, bf16[144,1152]{1,0:T(8,128)(2,1)S(1)} %get-tuple-element.18.we_ref, bf16[2240,768]{1,0:T(8,128)(2,1)S(1)} %bitcast.11, bf16[1152,768]{1,0:T(8,128)(2,1)S(1)} %bitcast.19, ...), custom_call_target="tpu_custom_call" | custom-call | flops 5898240000 | bytes 65536 | tf_op jit(solution)/shard_map/rest/pallas_call | solution.py:42
  30.9 2.5 %strips.1 = (bf16[2,26,16,384]{3,2,1,0:T(8,128)(2,1)S(1)}, bf16[2,26,16,384]{3,2,1,0:T(8,128)(2,1)S(1)}) custom-call(bf16[12,30,16,384]{3,2,1,0:T(8,128)(2,1)S(1)} %get-tuple-element.21.d_ref, bf16[12,29,16,384]{3,2,1,0:T(8,128)(2,1)S(1)} %get-tuple-element.22.s_ref, bf16[2,3,256,768]{3,2,1,0:T(8,128)(2,1)S(1)} %fold.1.w_ref, f32[1,192]{1,0:T(1,128)S(1)} %bitcast.16), custom_call_target="tpu_custom_call" | custom-call | flops 1962934272 | bytes 65536 | tf_op jit(solution)/shard_map/strips/pallas_call | solution.py:42
  33.5 0.0 collective-permute-done.2.fl_ref
  33.5 0.0 collective-permute-done.3.fr_ref
  33.5 0.7 %join.1 = (bf16[2,28,16,384]{3,2,1,0:T(8,128)(2,1)S(1)}, bf16[2,28,16,384]{3,2,1,0:T(8,128)(2,1)S(1)}) custom-call(s32[2]{0:T(128)S(1)} %pad_add_fusion.pos_ref, bf16[2,26,16,384]{3,2,1,0:T(8,128)(2,1)S(1)} %get-tuple-element.23.t_ref, bf16[2,26,16,384]{3,2,1,0:T(8,128)(2,1)S(1)} %get-tuple-element.24.l_ref, ...), custom_call_target="tpu_custom_call" | custom-call | flops 1048576 | bytes 65536 | tf_op jit(solution)/shard_map/join/pallas_call | solution.py:42
  34.2 4.1 %collective-permute-start.5 = (bf16[2,28,16,384]{3,2,1,0:T(8,128)(2,1)S(1)}, bf16[2,28,16,384]{3,2,1,0:T(8,128)(2,1)S(1)}, u32[]{:S(2)}, u32[]{:S(2)}) collective-permute-start(bf16[2,28,16,384]{3,2,1,0:T(8,128)(2,1)S(1)} %get-tuple-element.28), channel_id=1, source_target_pairs={{4,8},{12,16},{20,24},{28,32},{36,40},{44,48},{52,56},{60,64},{68,... | collective-permute-start | bytes 2064392 | tf_op jit(solution)/shard_map/ppermute | solution.py:28
  38.2 0.0 copy-start.3
  38.3 0.0 copy-start.4
  38.3 0.3 collective-permute-start.4
  38.6 9.0 %upper.1.u_ref = bf16[16,26,16,384]{3,2,1,0:T(8,128)(2,1)S(1)} custom-call(bf16[12,30,16,384]{3,2,1,0:T(8,128)(2,1)S(1)} %get-tuple-element.21.d_ref, bf16[12,29,16,384]{3,2,1,0:T(8,128)(2,1)S(1)} %get-tuple-element.22.s_ref, bf16[2,3,256,768]{3,2,1,0:T(8,128)(2,1)S(1)} %fold.1.w_ref, f32[1,192]{1,0:T(1,128)S(1)} %bitcast.17, ...), custom_call_target="tpu_custom_call" | custom-call | flops 7851737088 | bytes 65536 | tf_op jit(solution)/shard_map/upper/pallas_call | solution.py:42
  47.6 1.0 %collective-permute-done.5.odd_ref = bf16[2,28,16,384]{3,2,1,0:T(8,128)(2,1)S(1)} collective-permute-done((bf16[2,28,16,384]{3,2,1,0:T(8,128)(2,1)S(1)}, bf16[2,28,16,384]{3,2,1,0:T(8,128)(2,1)S(1)}, u32[]{:S(2)}, u32[]{:S(2)}) %collective-permute-start.5) | collective-permute-done | bytes 688160 | tf_op jit(solution)/shard_map/ppermute | solution.py:28
  48.5 0.0 collective-permute-done.4.even_ref
  48.5 0.0 copy-done.3
  48.5 0.0 copy-done.4
  48.5 3.7 %lower.1 = bf16[8,52,16,384]{3,2,1,0:T(8,128)(2,1)} custom-call(s32[2]{0:T(128)S(1)} %pad_add_fusion.pos_ref, s32[32]{0:T(128)S(1)} %copy-done.3, s32[4]{0:T(128)S(1)} %copy-done.4, bf16[16,26,16,384]{3,2,1,0:T(8,128)(2,1)S(1)} %upper.1.u_ref, bf16[10,2,16,384]{3,2,1,0:T(8,128)(2,1)S(1)} %collective-permute-done.2.fl_ref, ...), custom_call_target="tpu_custom_call" | custom-call | flops 1048576 | bytes 65536 | tf_op jit(solution)/shard_map/lower/pallas_call | solution.py:42
Async XLA Ops:
  1.1 10.5 %collective-permute-start.1 = (bf16[8,64,52]{2,1,0:T(8,128)(2,1)S(1)}, bf16[8,64,52]{2,1,0:T(8,128)(2,1)S(1)}, u32[]{:S(2)}, u32[]{:S(2)}) collective-permute-start(bf16[8,64,52]{2,1,0:T(8,128)(2,1)S(1)} %get-tuple-element.29), channel_id=1, source_target_pairs={{4,0},{8,4},{12,8},{16,12},{20,16},{24,20},{28,24},{32,28},{36,32}... | collective-permute-start | bytes 159752 | tf_op jit(solution)/shard_map/ppermute | solution.py:22
  5.7 8.4 %collective-permute-start = (bf16[8,64,52]{2,1,0:T(8,128)(2,1)S(1)}, bf16[8,64,52]{2,1,0:T(8,128)(2,1)S(1)}, u32[]{:S(2)}, u32[]{:S(2)}) collective-permute-start(bf16[8,64,52]{2,1,0:T(8,128)(2,1)S(1)} %get-tuple-element.30), channel_id=1, source_target_pairs={{0,4},{4,8},{8,12},{12,16},{16,20},{20,24},{24,28},{28,32},{32,36}... | collective-permute-start | bytes 159752 | tf_op jit(solution)/shard_map/ppermute | solution.py:22
  7.7 3.4 %copy-start = (bf16[3,3,384,192]{2,3,1,0:T(8,128)(2,1)S(1)}, bf16[3,3,384,192]{2,3,1,0:T(8,128)(2,1)}, u32[]{:S(2)}) copy-start(bf16[3,3,384,192]{2,3,1,0:T(8,128)(2,1)} %param.14) | copy-start | bytes 3981316
  11.0 3.1 %copy-start.1 = (bf16[8,208,64]{1,2,0:T(8,128)(2,1)S(1)}, bf16[8,208,64]{1,2,0:T(8,128)(2,1)}, u32[]{:S(2)}) copy-start(bf16[8,208,64]{1,2,0:T(8,128)(2,1)} %param.9) | copy-start | bytes 638980
  11.0 3.1 %copy-start.2 = (f32[192]{0:T(256)S(1)}, f32[192]{0:T(256)}, u32[]{:S(2)}) copy-start(f32[192]{0:T(256)} %param.15) | copy-start | bytes 2308
  11.1 3.1 %copy-start.5 = (bf16[3,384,768]{2,1,0:T(8,128)(2,1)S(1)}, bf16[3,384,768]{2,1,0:T(8,128)(2,1)}, u32[]{:S(2)}) copy-start(bf16[3,384,768]{2,1,0:T(8,128)(2,1)} %param.13) | copy-start | bytes 5308420
  11.1 3.1 %copy-start.6 = (bf16[8,2,10,28,16]{3,4,2,1,0:T(8,128)(2,1)S(1)}, bf16[8,2,10,28,16]{3,4,2,1,0:T(8,128)(2,1)}, u32[]{:S(2)}) copy-start(bf16[8,2,10,28,16]{3,4,2,1,0:T(8,128)(2,1)} %param.10) | copy-start | bytes 430084
  11.1 3.1 %copy-start.7 = (bf16[3,3,3,16,384]{4,3,2,1,0:T(8,128)(2,1)S(1)}, bf16[3,3,3,16,384]{4,3,2,1,0:T(8,128)(2,1)}, u32[]{:S(2)}) copy-start(bf16[3,3,3,16,384]{4,3,2,1,0:T(8,128)(2,1)} %ew_ref.1) | copy-start | bytes 995332
  18.7 14.8 %collective-permute-start.2 = (bf16[10,2,16,384]{3,2,1,0:T(8,128)(2,1)S(1)}, bf16[10,2,16,384]{3,2,1,0:T(8,128)(2,1)S(1)}, u32[]{:S(2)}, u32[]{:S(2)}) collective-permute-start(bf16[10,2,16,384]{3,2,1,0:T(8,128)(2,1)S(1)} %get-tuple-element.25), channel_id=1, source_target_pairs={{0,1},{1,2},{2,3},{4,5},{5,6},{6,7},{8,9},{9,10},{10,11},{12,13},{... | collective-permute-start | bytes 737288 | tf_op jit(solution)/shard_map/ppermute | solution.py:22
  22.5 10.9 %collective-permute-start.3 = (bf16[10,2,16,384]{3,2,1,0:T(8,128)(2,1)S(1)}, bf16[10,2,16,384]{3,2,1,0:T(8,128)(2,1)S(1)}, u32[]{:S(2)}, u32[]{:S(2)}) collective-permute-start(bf16[10,2,16,384]{3,2,1,0:T(8,128)(2,1)S(1)} %get-tuple-element.26), channel_id=1, source_target_pairs={{1,0},{2,1},{3,2},{5,4},{6,5},{7,6},{9,8},{10,9},{11,10},{13,12},{... | collective-permute-start | bytes 737288 | tf_op jit(solution)/shard_map/ppermute | solution.py:22
  34.2 14.4 %collective-permute-start.5 = (bf16[2,28,16,384]{3,2,1,0:T(8,128)(2,1)S(1)}, bf16[2,28,16,384]{3,2,1,0:T(8,128)(2,1)S(1)}, u32[]{:S(2)}, u32[]{:S(2)}) collective-permute-start(bf16[2,28,16,384]{3,2,1,0:T(8,128)(2,1)S(1)} %get-tuple-element.28), channel_id=1, source_target_pairs={{4,8},{12,16},{20,24},{28,32},{36,40},{44,48},{52,56},{60,64},{68,... | collective-permute-start | bytes 2064392 | tf_op jit(solution)/shard_map/ppermute | solution.py:28
  38.2 10.3 %copy-start.3 = (s32[32]{0:T(128)S(1)}, s32[32]{0:T(128)}, u32[]{:S(2)}) copy-start(s32[32]{0:T(128)} %rr_ref.1) | copy-start | bytes 388
  38.3 10.3 %copy-start.4 = (s32[4]{0:T(128)S(1)}, s32[4]{0:T(128)}, u32[]{:S(2)}) copy-start(s32[4]{0:T(128)} %cr_ref.1) | copy-start | bytes 52
  38.3 10.3 %collective-permute-start.4 = (bf16[2,28,16,384]{3,2,1,0:T(8,128)(2,1)S(1)}, bf16[2,28,16,384]{3,2,1,0:T(8,128)(2,1)S(1)}, u32[]{:S(2)}, u32[]{:S(2)}) collective-permute-start(bf16[2,28,16,384]{3,2,1,0:T(8,128)(2,1)S(1)} %get-tuple-element.27.after_ref), channel_id=1, source_target_pairs={{0,4},{8,12},{16,20},{24,28},{32,36},{40,44},{48,52},{56,60},{64,6... | collective-permute-start | bytes 2064392 | tf_op jit(solution)/shard_map/ppermute | solution.py:28

commit v3 on v2

--- a/solution.py
+++ b/solution.py
@@ -16,16 +16,14 @@
 NT = (((1,), (1,)), ((), ()))
 
 
-def shift(value, axis, step):
+def swap(value, axis, first):
     size = lax.axis_size(axis)
-    pairs = [(i, i + step) for i in range(size) if 0 <= i + step < size]
-    return lax.ppermute(value, axis, pairs)
-
-
-def swap(value, first):
-    size = lax.axis_size("rows")
     pairs = [(i, i + 1) for i in range(first, size - 1, 2)]
-    return lax.ppermute(value, "rows", pairs + [(j, i) for i, j in pairs])
+    return lax.ppermute(value, axis, pairs + [(j, i) for i, j in pairs])
+
+
+def either(pos, even, odd, rows):
+    return jnp.where(jnp.full((rows, 1), pos % 2, jnp.int32) == 0, even, odd)
 
 
 VM = pl.BlockSpec(memory_space=pltpu.VMEM)
@@ -56,15 +54,21 @@
 STEPS = 5
 
 
-def gather_body(col, tok_ref, before_ref, after_ref, cache_ref, x_ref, t_ref, lat_ref, old_ref):
-    lat_ref[...] = jnp.zeros(lat_ref.shape, F32)
-    old_ref[...] = jnp.zeros(old_ref.shape, F32)
+def gather_body(row, col, tok_ref, even_ref, odd_ref, cache_ref, x_ref, t_ref, lat_ref, old_ref):
+    for ref in (lat_ref, old_ref):
+        for e in (0, TR + 1):
+            ref[e * WIDE : (e + 1) * WIDE, :] = jnp.zeros((WIDE, 128), F32)
+        for e in range(1, TR + 1):
+            for u in (0, TC + 1):
+                at = e * WIDE + u * VID
+                ref[at : at + VID, :] = jnp.zeros((VID, 128), F32)
     t_ref[...] = jnp.zeros(t_ref.shape, F32)
     for v in range(VID):
         own = jnp.transpose(tok_ref[v].astype(F32))
-        rows = [jnp.transpose(before_ref[v].astype(F32))]
+        by_even, by_odd = even_ref[v].astype(F32), odd_ref[v].astype(F32)
+        rows = [jnp.transpose(either(row, by_odd, by_even, 64))]
         rows += [own[52 * i : 52 * (i + 1)] for i in range(4)]
-        rows += [jnp.transpose(after_ref[v].astype(F32))]
+        rows += [jnp.transpose(either(row, by_even, by_odd, 64))]
         for i in range(6):
             t_ref[v % 2, pl.ds(i * PITCH + 1, 52), 0:64] = rows[i]
         for i in range(6):
@@ -126,8 +130,8 @@
     we_ref,
     dl_ref,
     dr_ref,
-    left_ref,
-    right_ref,
+    even_ref,
+    odd_ref,
     t_ref,
     lat_ref,
     old_ref,
@@ -141,7 +145,7 @@
             for kc in range(3):
                 at = (kr * 3 + f) * 16
                 we_ref[at : at + 16, kc * C : (kc + 1) * C] = ew_ref[f, kr, kc]
-    gather_body(pos_ref[1], tok_ref, before_ref, after_ref, cache_ref, x_ref, t_ref, lat_ref, old_ref)
+    gather_body(pos_ref[0], pos_ref[1], tok_ref, before_ref, after_ref, cache_ref, x_ref, t_ref, lat_ref, old_ref)
     d = mixed(x_ref, we_ref, cm_ref, wt_ref, ((0, TR, 0, 2), (0, TR, TC - 2, 2)))
     dl_ref[1 : TR + 1, 1:3] = d[: 2 * TR].reshape(TR, 2, 2 * VID, C)
     dr_ref[1 : TR + 1, 0:2] = d[2 * TR :].reshape(TR, 2, 2 * VID, C)
@@ -150,8 +154,8 @@
     gain = half_gain(gain_ref)
     for a in range(2):
         v = both(w_ref, gain, ((dl_ref, sl_ref, 0, TR, 0, 1), (dr_ref, sr_ref, 0, TR, 0, 1)), a)
-        left_ref[:, a] = v[:TR]
-        right_ref[:, a] = v[TR:]
+        even_ref[:, a] = either(pos_ref[1], v[TR:].astype(F32), v[:TR].astype(F32), 2 * VID).astype(BF)
+        odd_ref[:, a] = either(pos_ref[1], v[:TR].astype(F32), v[TR:].astype(F32), 2 * VID).astype(BF)
 
 
 def edge(pos, tok, before, after, cache, ew, cm, wt, w, gain):
@@ -279,15 +283,16 @@
     return call(strips_body, "strips", (strip, strip), (d, s, w, gain), 2 * 832 * 18 * 65536)
 
 
-def join_body(pos_ref, t_ref, l_ref, fl_ref, fr_ref, even_ref, odd_ref):
+def join_body(pos_ref, t_ref, l_ref, se_ref, so_ref, even_ref, odd_ref):
     n = TC - 2
     even = pos_ref[0] % 2 == 0
 
     def put(ref, own_ref, i):
         ref[:, 1 : n + 1] = own_ref[...]
         for a in range(2):
-            ref[a, 0] = fl_ref[i, a]
-            ref[a, n + 1] = fr_ref[i, a]
+            by_even, by_odd = se_ref[i, a].astype(F32), so_ref[i, a].astype(F32)
+            ref[a, 0] = either(pos_ref[1], by_odd, by_even, 2 * VID).astype(BF)
+            ref[a, n + 1] = either(pos_ref[1], by_even, by_odd, 2 * VID).astype(BF)
 
     @pl.when(even)
     def _():
@@ -332,18 +337,23 @@
 GROUP = 2
 
 
-def lower_body(pos_ref, rr_ref, cr_ref, u_ref, fl_ref, fr_ref, even_ref, odd_ref, o_ref, buf, sem):
+def lower_body(pos_ref, rr_ref, cr_ref, u_ref, se_ref, so_ref, even_ref, odd_ref, o_ref, buf, sem):
     r, c = pos_ref[0], pos_ref[1]
     up = [ramp(r, rr_ref, ROWS, p) for p in (0, 1)]
     down = [ramp(r + 1, rr_ref, ROWS, p) for p in (-2, -1)]
     groups = (TC - 2) // GROUP
-    even = jnp.full((2 * VID, 1), r % 2, jnp.int32) == 0
 
     def above(p, j):
-        return jnp.where(even, odd_ref[p, j].astype(F32), even_ref[p, j].astype(F32))
+        return either(r, odd_ref[p, j].astype(F32), even_ref[p, j].astype(F32), 2 * VID)
 
     def below(p, j):
-        return jnp.where(even, even_ref[p, j].astype(F32), odd_ref[p, j].astype(F32))
+        return either(r, even_ref[p, j].astype(F32), odd_ref[p, j].astype(F32), 2 * VID)
+
+    def left(i, a):
+        return either(c, so_ref[i, a].astype(F32), se_ref[i, a].astype(F32), 2 * VID)
+
+    def right(i, a):
+        return either(c, se_ref[i, a].astype(F32), so_ref[i, a].astype(F32), 2 * VID)
 
     def sends(g):
         at = pl.ds(g * 2 * GROUP, 2 * GROUP)
@@ -369,7 +379,7 @@
             rows.append(v[None])
         put(j, jnp.concatenate(rows, axis=0))
 
-    def outer(j, side_ref, slot, w):
+    def outer(j, side, slot, w):
         first = lax.broadcasted_iota(jnp.int32, (2 * VID, 1), 0) < VID
         w = jnp.where(first, w[0], w[1])
 
@@ -378,7 +388,7 @@
 
         rows = []
         for p in range(16):
-            v = across(rows_of(j, p), side_ref[1 + p // 2, p % 2])
+            v = across(rows_of(j, p), side(1 + p // 2, p % 2))
             if p < 2:
                 v = v * up[p] + across(above(p, j + 1), above(p, slot)) * (1.0 - up[p])
             elif p > 13:
@@ -387,7 +397,7 @@
             rows.append(v.astype(BF)[None])
         put(j, jnp.concatenate(rows, axis=0))
 
-    outer(0, fl_ref, 0, [1.0 - ramp(c, cr_ref, COLS, x) for x in (0, 1)])
+    outer(0, left, 0, [1.0 - ramp(c, cr_ref, COLS, x) for x in (0, 1)])
     for j in range(1, GROUP):
         inner(j)
     sends(0).start()
@@ -401,7 +411,7 @@
     lax.fori_loop(1, groups - 1, step, 0)
     for j in range(TC - 2 - GROUP, TC - 3):
         inner(j)
-    outer(TC - 3, fr_ref, TC - 1, [ramp(c + 1, cr_ref, COLS, x) for x in (-2, -1)])
+    outer(TC - 3, right, TC - 1, [ramp(c + 1, cr_ref, COLS, x) for x in (-2, -1)])
     sends(groups - 1).start()
     for g in range(groups):
         sends(g).wait()
@@ -438,8 +448,10 @@
     row_pos = lax.axis_index("rows")
     col_pos = lax.axis_index("cols")
     tok = jnp.transpose(latent_tokens, (0, 2, 1))
-    before = shift(tok[:, :, 156:], "rows", 1)
-    after = shift(tok[:, :, :52], "rows", -1)
+    first, last = tok[:, :, :52], tok[:, :, 156:]
+    even = row_pos % 2 == 0
+    by_odd = swap(jnp.where(even, first, last), "rows", 1)
+    by_even = swap(jnp.where(even, last, first), "rows", 0)
     cache = jnp.transpose(cache_latent, (0, 1, 2, 4, 3))
     cm = jnp.transpose(cache_middle, (2, 3, 0, 1, 4)).reshape(TR * TC * VID, 2 * C)
     wt = time_weight.reshape(3 * C, 2 * C)
@@ -447,15 +459,15 @@
     gain = norm_gain.reshape(1, U)
     pos = jnp.stack([row_pos, col_pos]).astype(jnp.int32)
     w = fold(ut)
-    x, we, dl, dr, left, right = edge(pos, tok, before, after, cache, entry_weight, cm, wt, w, gain)
-    from_left = shift(right, "cols", 1)
-    from_right = shift(left, "cols", -1)
+    x, we, dl, dr, side_even, side_odd = edge(pos, tok, by_even, by_odd, cache, entry_weight, cm, wt, w, gain)
+    side_even = swap(side_even, "cols", 0)
+    side_odd = swap(side_odd, "cols", 1)
     d, s = rest(x, we, cm, wt, dl, dr)
-    to_even, to_odd = join(pos, *strips(d, s, w, gain), from_left, from_right)
-    by_odd = swap(to_odd, 1)
-    by_even = swap(to_even, 0)
+    to_even, to_odd = join(pos, *strips(d, s, w, gain), side_even, side_odd)
+    by_odd = swap(to_odd, "rows", 1)
+    by_even = swap(to_even, "rows", 0)
     u = upper(d, s, w, gain, to_even)
-    out = lower(pos, row_ramp, col_ramp, u, from_left, from_right, by_even, by_odd)
+    out = lower(pos, row_ramp, col_ramp, u, side_even, side_odd, by_even, by_odd)
     return jnp.transpose(out, (0, 2, 1, 3))
 
 

time: 52.7 us -> 49 us (0.930)
  starting transfers between devices: 17 us -> 13.3 us
  other arithmetic: 0.08 us -> 1.15 us
  waiting for transfers between devices: 3.49 us -> 2.73 us
    ppermute x6, starting transfers between devices: 17 us -> 13.3 us  [swap(): return lax.ppermute(value, axis, pairs + [(j, i) for i, j in pairs])]
    unnamed x16, local copies, waits for them, and re-layouts: 0.05 us -> 1.29 us
    select_n x0 -> x1, other arithmetic: none -> 1.07 us  [per_device(): by_odd = swap(jnp.where(even, first, last), 'rows', 1)]
    slice x1 -> x0, local copies, waits for them, and re-layouts: 1.07 us -> none  [per_device(): after = shift(tok[:, :, :52], 'rows', -1)]
    ppermute x6, waiting for transfers between devices: 3.49 us -> 2.73 us  [swap(): return lax.ppermute(value, axis, pairs + [(j, i) for i, j in pairs])]
  transfers between devices with their start and end apart: 6 -> 6, of which waited for: 2 -> 1; matrix products, arithmetic and copies ran while one was open for 6% -> 7% of each run, Pallas kernels for 35% -> 36%
where the time goes in v3:
time: 49 us; the launch traced here: 48.8 us
  Pallas kernels  26.6 us (54%)
  starting transfers between devices  13.3 us (27%)
  local copies, waits for them, and re-layouts  4.59 us (9%)
  waiting for transfers between devices  2.73 us (6%)
  other arithmetic  1.15 us (2%)
    pallas_call x7, Pallas kernels, call(): pl.pallas_call(body, in_specs=specs, out_specs=jax.tree.map(lambda _: VM,...  26.6 us
    ppermute x6, starting transfers between devices, swap(): return lax.ppermute(value, axis, pairs + [(j, i) for i, j in pairs])  13.3 us
    transpose x1, local copies, waits for them, and re-layouts, per_device(): jnp.transpose(cache_middle, (2, 3, 0, 1, 4)).reshape(TR * TC * VID, 2 * C)  3.3 us
    ppermute x6, waiting for transfers between devices, swap(): return lax.ppermute(value, axis, pairs + [(j, i) for i, j in pairs])  2.73 us
    unnamed x16, local copies, waits for them, and re-layouts  1.29 us
    select_n x1, other arithmetic, per_device(): by_odd = swap(jnp.where(even, first, last), 'rows', 1)  1.07 us
  transfers between devices with their start and end apart: 6, of which 1 were waited for; matrix products, arithmetic and copies ran while one was open for 7% of the time, Pallas kernels for 36%

profile of v3, /device:TPU:38, one launch (start us, length us, event | category | flops | bytes accessed | tf_op | source)
XLA Modules:
  0.0 48.8 jit_solution(3478573961032723482)
XLA Ops:
  0.0 1.1 %broadcast_select_fusion = (bf16[8,64,52]{2,1,0:T(8,128)(2,1)S(1)}, bf16[8,64,52]{2,1,0:T(8,128)(2,1)S(1)}) fusion(pred[]{:T(512)S(6)} %eq.5, bf16[8,64,208]{2,1,0:T(8,128)(2,1)} %bitcast.13), kind=kLoop, calls=%fused_computation | loop fusion | flops 53248 | bytes 212993 | tf_op jit(solution)/shard_map/jit(_where)/select_n | solution.py:453
  1.1 4.6 %collective-permute-start.1 = (bf16[8,64,52]{2,1,0:T(8,128)(2,1)S(1)}, bf16[8,64,52]{2,1,0:T(8,128)(2,1)S(1)}, u32[]{:S(2)}, u32[]{:S(2)}) collective-permute-start(bf16[8,64,52]{2,1,0:T(8,128)(2,1)S(1)} %get-tuple-element.29), channel_id=1, source_target_pairs={{4,8},{12,16},{20,24},{28,32},{36,40},{44,48},{52,56},{60,64},{68,... | collective-permute-start | bytes 159752 | tf_op jit(solution)/shard_map/ppermute | solution.py:22
  5.7 0.1 collective-permute-start
  5.8 0.1 pad_add_fusion.pos_ref
  5.9 0.0 copy-start
  5.9 3.3 %copy.10 = bf16[10,28,8,2,384]{4,2,3,1,0:T(8,128)(2,1)S(1)} copy(bf16[10,28,8,2,384]{4,3,1,0,2:T(2,128)(2,1)} %bitcast.21) | data formatting | bytes 6881280 | tf_op jit(solution)/shard_map/transpose | solution.py:456
  9.2 0.0 copy-start.1
  9.2 0.0 copy-start.2
  9.2 0.0 copy-start.5
  9.2 0.0 copy-start.6
  9.2 0.0 copy-start.7
  9.3 0.0 copy-done
  9.3 0.5 fold.1.w_ref
  9.7 0.0 collective-permute-done.1.after_ref
  9.7 0.0 collective-permute-done.before_ref
  9.8 0.4 copy-done.1
  10.1 0.0 copy-done.2
  10.1 0.6 %copy-done.5 = bf16[3,384,768]{2,1,0:T(8,128)(2,1)S(1)} copy-done((bf16[3,384,768]{2,1,0:T(8,128)(2,1)S(1)}, bf16[3,384,768]{2,1,0:T(8,128)(2,1)}, u32[]{:S(2)}) %copy-start.5) | copy-done | bytes 1769496
  10.8 0.1 copy-done.6
  10.9 0.1 copy-done.7
  11.0 4.4 %edge.1 = (bf16[2880,128]{1,0:T(8,128)(2,1)S(1)}, bf16[144,1152]{1,0:T(8,128)(2,1)S(1)}, bf16[12,3,16,384]{3,2,1,0:T(8,128)(2,1)S(1)}, bf16[12,3,16,384]{3,2,1,0...) custom-call(s32[2]{0:T(128)S(1)} %pad_add_fusion.pos_ref, ...), custom_call_target="tpu_custom_call" | custom-call | flops 5242880000 | bytes 65536 | tf_op jit(solution)/shard_map/edge/pallas_call | solution.py:40
  15.5 0.2 collective-permute-start.2
  15.6 5.5 %collective-permute-start.3 = (bf16[10,2,16,384]{3,2,1,0:T(8,128)(2,1)S(1)}, bf16[10,2,16,384]{3,2,1,0:T(8,128)(2,1)S(1)}, u32[]{:S(2)}, u32[]{:S(2)}) collective-permute-start(bf16[10,2,16,384]{3,2,1,0:T(8,128)(2,1)S(1)} %get-tuple-element.26), channel_id=1, source_target_pairs={{1,2},{2,1},{5,6},{6,5},{9,10},{10,9},{13,14},{14,13},{17,18},{18,... | collective-permute-start | bytes 737288 | tf_op jit(solution)/shard_map/ppermute | solution.py:22
  21.2 6.1 %rest.1 = (bf16[12,30,16,384]{3,2,1,0:T(8,128)(2,1)S(1)}, bf16[12,29,16,384]{3,2,1,0:T(8,128)(2,1)S(1)}) custom-call(bf16[2880,128]{1,0:T(8,128)(2,1)S(1)} %get-tuple-element.17.x_ref, bf16[144,1152]{1,0:T(8,128)(2,1)S(1)} %get-tuple-element.18.we_ref, bf16[2240,768]{1,0:T(8,128)(2,1)S(1)} %bitcast.11, bf16[1152,768]{1,0:T(8,128)(2,1)S(1)} %bitcast.19, ...), custom_call_target="tpu_custom_call" | custom-call | flops 5898240000 | bytes 65536 | tf_op jit(solution)/shard_map/rest/pallas_call | solution.py:40
  27.3 2.5 %strips.1 = (bf16[2,26,16,384]{3,2,1,0:T(8,128)(2,1)S(1)}, bf16[2,26,16,384]{3,2,1,0:T(8,128)(2,1)S(1)}) custom-call(bf16[12,30,16,384]{3,2,1,0:T(8,128)(2,1)S(1)} %get-tuple-element.21.d_ref, bf16[12,29,16,384]{3,2,1,0:T(8,128)(2,1)S(1)} %get-tuple-element.22.s_ref, bf16[2,3,256,768]{3,2,1,0:T(8,128)(2,1)S(1)} %fold.1.w_ref, f32[1,192]{1,0:T(1,128)S(1)} %bitcast.16), custom_call_target="tpu_custom_call" | custom-call | flops 1962934272 | bytes 65536 | tf_op jit(solution)/shard_map/strips/pallas_call | solution.py:40
  29.8 0.0 collective-permute-done.2.se_ref
  29.8 0.0 collective-permute-done.3.so_ref
  29.8 0.7 %join.1 = (bf16[2,28,16,384]{3,2,1,0:T(8,128)(2,1)S(1)}, bf16[2,28,16,384]{3,2,1,0:T(8,128)(2,1)S(1)}) custom-call(s32[2]{0:T(128)S(1)} %pad_add_fusion.pos_ref, bf16[2,26,16,384]{3,2,1,0:T(8,128)(2,1)S(1)} %get-tuple-element.23.t_ref, bf16[2,26,16,384]{3,2,1,0:T(8,128)(2,1)S(1)} %get-tuple-element.24.l_ref, ...), custom_call_target="tpu_custom_call" | custom-call | flops 1048576 | bytes 65536 | tf_op jit(solution)/shard_map/join/pallas_call | solution.py:40
  30.5 2.6 %collective-permute-start.5 = (bf16[2,28,16,384]{3,2,1,0:T(8,128)(2,1)S(1)}, bf16[2,28,16,384]{3,2,1,0:T(8,128)(2,1)S(1)}, u32[]{:S(2)}, u32[]{:S(2)}) collective-permute-start(bf16[2,28,16,384]{3,2,1,0:T(8,128)(2,1)S(1)} %get-tuple-element.28), channel_id=1, source_target_pairs={{4,8},{12,16},{20,24},{28,32},{36,40},{44,48},{52,56},{60,64},{68,... | collective-permute-start | bytes 2064392 | tf_op jit(solution)/shard_map/ppermute | solution.py:22
  33.1 0.0 copy-start.3
  33.1 0.0 copy-start.4
  33.1 0.3 collective-permute-start.4
  33.4 8.7 %upper.1.u_ref = bf16[16,26,16,384]{3,2,1,0:T(8,128)(2,1)S(1)} custom-call(bf16[12,30,16,384]{3,2,1,0:T(8,128)(2,1)S(1)} %get-tuple-element.21.d_ref, bf16[12,29,16,384]{3,2,1,0:T(8,128)(2,1)S(1)} %get-tuple-element.22.s_ref, bf16[2,3,256,768]{3,2,1,0:T(8,128)(2,1)S(1)} %fold.1.w_ref, f32[1,192]{1,0:T(1,128)S(1)} %bitcast.17, ...), custom_call_target="tpu_custom_call" | custom-call | flops 7851737088 | bytes 65536 | tf_op jit(solution)/shard_map/upper/pallas_call | solution.py:40
  42.1 2.7 %collective-permute-done.5.odd_ref = bf16[2,28,16,384]{3,2,1,0:T(8,128)(2,1)S(1)} collective-permute-done((bf16[2,28,16,384]{3,2,1,0:T(8,128)(2,1)S(1)}, bf16[2,28,16,384]{3,2,1,0:T(8,128)(2,1)S(1)}, u32[]{:S(2)}, u32[]{:S(2)}) %collective-permute-start.5) | collective-permute-done | bytes 688160 | tf_op jit(solution)/shard_map/ppermute | solution.py:22
  44.8 0.0 collective-permute-done.4.even_ref
  44.8 0.0 copy-done.3
  44.8 0.0 copy-done.4
  44.9 3.7 %lower.1 = bf16[8,52,16,384]{3,2,1,0:T(8,128)(2,1)} custom-call(s32[2]{0:T(128)S(1)} %pad_add_fusion.pos_ref, s32[32]{0:T(128)S(1)} %copy-done.3, s32[4]{0:T(128)S(1)} %copy-done.4, bf16[16,26,16,384]{3,2,1,0:T(8,128)(2,1)S(1)} %upper.1.u_ref, bf16[10,2,16,384]{3,2,1,0:T(8,128)(2,1)S(1)} %collective-permute-done.2.se_ref, ...), custom_call_target="tpu_custom_call" | custom-call | flops 1048576 | bytes 65536 | tf_op jit(solution)/shard_map/lower/pallas_call | solution.py:40
Async XLA Ops:
  1.1 8.7 %collective-permute-start.1 = (bf16[8,64,52]{2,1,0:T(8,128)(2,1)S(1)}, bf16[8,64,52]{2,1,0:T(8,128)(2,1)S(1)}, u32[]{:S(2)}, u32[]{:S(2)}) collective-permute-start(bf16[8,64,52]{2,1,0:T(8,128)(2,1)S(1)} %get-tuple-element.29), channel_id=1, source_target_pairs={{4,8},{12,16},{20,24},{28,32},{36,40},{44,48},{52,56},{60,64},{68,... | collective-permute-start | bytes 159752 | tf_op jit(solution)/shard_map/ppermute | solution.py:22
  5.7 4.0 %collective-permute-start = (bf16[8,64,52]{2,1,0:T(8,128)(2,1)S(1)}, bf16[8,64,52]{2,1,0:T(8,128)(2,1)S(1)}, u32[]{:S(2)}, u32[]{:S(2)}) collective-permute-start(bf16[8,64,52]{2,1,0:T(8,128)(2,1)S(1)} %get-tuple-element.30), channel_id=1, source_target_pairs={{0,4},{8,12},{16,20},{24,28},{32,36},{40,44},{48,52},{56,60},{64,6... | collective-permute-start | bytes 159752 | tf_op jit(solution)/shard_map/ppermute | solution.py:22
  5.9 3.4 %copy-start = (bf16[3,3,384,192]{2,3,1,0:T(8,128)(2,1)S(1)}, bf16[3,3,384,192]{2,3,1,0:T(8,128)(2,1)}, u32[]{:S(2)}) copy-start(bf16[3,3,384,192]{2,3,1,0:T(8,128)(2,1)} %param.14) | copy-start | bytes 3981316
  9.2 1.0 %copy-start.1 = (bf16[8,208,64]{1,2,0:T(8,128)(2,1)S(1)}, bf16[8,208,64]{1,2,0:T(8,128)(2,1)}, u32[]{:S(2)}) copy-start(bf16[8,208,64]{1,2,0:T(8,128)(2,1)} %param.9) | copy-start | bytes 638980
  9.2 0.9 %copy-start.2 = (f32[192]{0:T(256)S(1)}, f32[192]{0:T(256)}, u32[]{:S(2)}) copy-start(f32[192]{0:T(256)} %param.15) | copy-start | bytes 2308
  9.2 1.6 %copy-start.5 = (bf16[3,384,768]{2,1,0:T(8,128)(2,1)S(1)}, bf16[3,384,768]{2,1,0:T(8,128)(2,1)}, u32[]{:S(2)}) copy-start(bf16[3,384,768]{2,1,0:T(8,128)(2,1)} %param.13) | copy-start | bytes 5308420
  9.2 1.7 %copy-start.6 = (bf16[8,2,10,28,16]{3,4,2,1,0:T(8,128)(2,1)S(1)}, bf16[8,2,10,28,16]{3,4,2,1,0:T(8,128)(2,1)}, u32[]{:S(2)}) copy-start(bf16[8,2,10,28,16]{3,4,2,1,0:T(8,128)(2,1)} %param.10) | copy-start | bytes 430084
  9.2 1.8 %copy-start.7 = (bf16[3,3,3,16,384]{4,3,2,1,0:T(8,128)(2,1)S(1)}, bf16[3,3,3,16,384]{4,3,2,1,0:T(8,128)(2,1)}, u32[]{:S(2)}) copy-start(bf16[3,3,3,16,384]{4,3,2,1,0:T(8,128)(2,1)} %ew_ref.1) | copy-start | bytes 995332
  15.5 14.3 %collective-permute-start.2 = (bf16[10,2,16,384]{3,2,1,0:T(8,128)(2,1)S(1)}, bf16[10,2,16,384]{3,2,1,0:T(8,128)(2,1)S(1)}, u32[]{:S(2)}, u32[]{:S(2)}) collective-permute-start(bf16[10,2,16,384]{3,2,1,0:T(8,128)(2,1)S(1)} %get-tuple-element.25), channel_id=1, source_target_pairs={{0,1},{2,3},{1,0},{3,2},{4,5},{6,7},{5,4},{7,6},{8,9},{10,11},{9,8... | collective-permute-start | bytes 737288 | tf_op jit(solution)/shard_map/ppermute | solution.py:22
  15.6 14.1 %collective-permute-start.3 = (bf16[10,2,16,384]{3,2,1,0:T(8,128)(2,1)S(1)}, bf16[10,2,16,384]{3,2,1,0:T(8,128)(2,1)S(1)}, u32[]{:S(2)}, u32[]{:S(2)}) collective-permute-start(bf16[10,2,16,384]{3,2,1,0:T(8,128)(2,1)S(1)} %get-tuple-element.26), channel_id=1, source_target_pairs={{1,2},{2,1},{5,6},{6,5},{9,10},{10,9},{13,14},{14,13},{17,18},{18,... | collective-permute-start | bytes 737288 | tf_op jit(solution)/shard_map/ppermute | solution.py:22
  30.5 14.4 %collective-permute-start.5 = (bf16[2,28,16,384]{3,2,1,0:T(8,128)(2,1)S(1)}, bf16[2,28,16,384]{3,2,1,0:T(8,128)(2,1)S(1)}, u32[]{:S(2)}, u32[]{:S(2)}) collective-permute-start(bf16[2,28,16,384]{3,2,1,0:T(8,128)(2,1)S(1)} %get-tuple-element.28), channel_id=1, source_target_pairs={{4,8},{12,16},{20,24},{28,32},{36,40},{44,48},{52,56},{60,64},{68,... | collective-permute-start | bytes 2064392 | tf_op jit(solution)/shard_map/ppermute | solution.py:22
  33.1 11.8 %copy-start.3 = (s32[32]{0:T(128)S(1)}, s32[32]{0:T(128)}, u32[]{:S(2)}) copy-start(s32[32]{0:T(128)} %rr_ref.1) | copy-start | bytes 388
  33.1 11.8 %copy-start.4 = (s32[4]{0:T(128)S(1)}, s32[4]{0:T(128)}, u32[]{:S(2)}) copy-start(s32[4]{0:T(128)} %cr_ref.1) | copy-start | bytes 52
  33.1 11.8 %collective-permute-start.4 = (bf16[2,28,16,384]{3,2,1,0:T(8,128)(2,1)S(1)}, bf16[2,28,16,384]{3,2,1,0:T(8,128)(2,1)S(1)}, u32[]{:S(2)}, u32[]{:S(2)}) collective-permute-start(bf16[2,28,16,384]{3,2,1,0:T(8,128)(2,1)S(1)} %get-tuple-element.27.after_ref), channel_id=1, source_target_pairs={{0,4},{8,12},{16,20},{24,28},{32,36},{40,44},{48,52},{56,60},{64,6... | collective-permute-start | bytes 2064392 | tf_op jit(solution)/shard_map/ppermute | solution.py:22

commit v4 on v3

--- a/solution.py
+++ b/solution.py
@@ -51,7 +51,6 @@
 
 WIDE = (TC + 2) * VID
 PITCH = 56
-STEPS = 5
 
 
 def gather_body(row, col, tok_ref, even_ref, odd_ref, cache_ref, x_ref, t_ref, lat_ref, old_ref):
@@ -179,26 +178,38 @@
     )
 
 
-def rest_body(x_ref, we_ref, cm_ref, wt_ref, dl_ref, dr_ref, d_ref, s_ref):
+def ends_body(x_ref, we_ref, cm_ref, wt_ref, dl_ref, dr_ref, td_ref, ts_ref, ld_ref, ls_ref):
     n = TC - 4
-    line = jnp.zeros((1, n, 2 * VID, C), BF)
-    d_ref[0:1, 3 : n + 3] = line
-    d_ref[TR + 1 : TR + 2, 3 : n + 3] = line
-    d_ref[:, 0:3] = dl_ref[...]
-    d_ref[:, n + 3 : n + 6] = dr_ref[...]
-    for i in (0, TR + 1):
-        s_ref[i] = jnp.zeros((TC + 1, 2 * VID, C), BF)
-    rows = TR // STEPS
-    for g in range(STEPS):
-        d = mixed(x_ref, we_ref, cm_ref, wt_ref, ((g * rows, rows, 2, n),))
-        d_ref[1 + g * rows : 1 + (g + 1) * rows, 3 : n + 3] = d.reshape(rows, n, 2 * VID, C)
-        for i in range(1 + g * rows, 1 + (g + 1) * rows):
+    for d_ref, s_ref, first, line, row in ((td_ref, ts_ref, 0, 0, 0), (ld_ref, ls_ref, TR - 1, 2, TR - 2)):
+        d_ref[line, 3 : n + 3] = jnp.zeros((n, 2 * VID, C), BF)
+        d_ref[:, 0:3] = dl_ref[first : first + 3]
+        d_ref[:, n + 3 : n + 6] = dr_ref[first : first + 3]
+        d = mixed(x_ref, we_ref, cm_ref, wt_ref, ((row, 2, 2, n),))
+        at = 1 if line == 0 else 0
+        d_ref[at : at + 2, 3 : n + 3] = d.reshape(2, n, 2 * VID, C)
+        for i in range(3):
             s_ref[i : i + 1] = steps_right(d_ref[i : i + 1])
 
 
-def rest(x, we, cm, wt, dl, dr):
-    outs = (pltpu.VMEM((TR + 2, TC + 2, 2 * VID, C), BF), pltpu.VMEM((TR + 2, TC + 1, 2 * VID, C), BF))
-    return call(rest_body, "rest", outs, (x, we, cm, wt, dl, dr), 2 * 45000 * 65536)
+def ends(x, we, cm, wt, dl, dr):
+    part = pltpu.VMEM((3, TC + 2, 2 * VID, C), BF)
+    step = pltpu.VMEM((3, TC + 1, 2 * VID, C), BF)
+    return call(ends_body, "ends", (part, step, part, step), (x, we, cm, wt, dl, dr), 2 * 18000 * 65536)
+
+
+def rest_body(x_ref, we_ref, cm_ref, wt_ref, dl_ref, dr_ref, td_ref, ts_ref, ld_ref, ls_ref, d_ref, s_ref):
+    n = TC - 4
+    d_ref[0:3] = td_ref[...]
+    s_ref[0:3] = ts_ref[...]
+    d_ref[TR - 1 : TR + 2] = ld_ref[...]
+    s_ref[TR - 1 : TR + 2] = ls_ref[...]
+    d_ref[3 : TR - 1, 0:3] = dl_ref[3 : TR - 1]
+    d_ref[3 : TR - 1, n + 3 : n + 6] = dr_ref[3 : TR - 1]
+    for row in range(2, TR - 2, 2):
+        d = mixed(x_ref, we_ref, cm_ref, wt_ref, ((row, 2, 2, n),))
+        d_ref[1 + row : 3 + row, 3 : n + 3] = d.reshape(2, n, 2 * VID, C)
+        for i in range(1 + row, 3 + row):
+            s_ref[i : i + 1] = steps_right(d_ref[i : i + 1])
 
 
 def fold_body(ut_ref, w_ref):
@@ -270,17 +281,17 @@
     return jnp.concatenate([g, g[:, :64], g[:, 128:], g[:, 64:128]], axis=1)
 
 
-def strips_body(d_ref, s_ref, w_ref, gain_ref, top_ref, low_ref):
+def strips_body(td_ref, ts_ref, ld_ref, ls_ref, w_ref, gain_ref, top_ref, low_ref):
     gain = half_gain(gain_ref)
     n = TC - 2
     for a in range(2):
-        for i, ref in ((0, top_ref), (TR - 1, low_ref)):
-            ref[a] = both(w_ref, gain, ((d_ref, s_ref, i, 1, 1, n),), a)
-
-
-def strips(d, s, w, gain):
+        for d_ref, s_ref, ref in ((td_ref, ts_ref, top_ref), (ld_ref, ls_ref, low_ref)):
+            ref[a] = both(w_ref, gain, ((d_ref, s_ref, 0, 1, 1, n),), a)
+
+
+def strips(rows, w, gain):
     strip = pltpu.VMEM((2, TC - 2, 2 * VID, 2 * U), BF)
-    return call(strips_body, "strips", (strip, strip), (d, s, w, gain), 2 * 832 * 18 * 65536)
+    return call(strips_body, "strips", (strip, strip), (*rows, w, gain), 2 * 832 * 18 * 65536)
 
 
 def join_body(pos_ref, t_ref, l_ref, se_ref, so_ref, even_ref, odd_ref):
@@ -310,22 +321,27 @@
     return call(join_body, "join", (strip, strip), (pos, t, l, fl, fr), 1 << 20, smem=1)
 
 
-CHUNK = 26
-
-
-def upper_body(d_ref, s_ref, w_ref, gain_ref, after_ref, o_ref):
-    del after_ref
+def upper_body(*refs):
+    parts, (w_ref, gain_ref, _, o_ref, d_ref, s_ref) = refs[:10], refs[10:]
+    rest_body(*parts, d_ref, s_ref)
     gain = half_gain(gain_ref)
     for i in range(TR - 2):
         for a in range(2):
-            for j in range(0, TC - 2, CHUNK):
-                area = (d_ref, s_ref, i + 1, 1, 1 + j, CHUNK)
-                o_ref[2 * i + a, j : j + CHUNK] = both(w_ref, gain, (area,), a)
-
-
-def upper(d, s, w, gain, after):
-    out = pltpu.VMEM((2 * (TR - 2), TC - 2, 2 * VID, 2 * U), BF)
-    return call(upper_body, "upper", out, (d, s, w, gain, after), 2 * (TR - 2) * 416 * 18 * 65536)
+            o_ref[2 * i + a] = both(w_ref, gain, ((d_ref, s_ref, i + 1, 1, 1, TC - 2),), a)
+
+
+def upper(parts, w, gain, after):
+    return call(
+        upper_body,
+        "upper",
+        pltpu.VMEM((2 * (TR - 2), TC - 2, 2 * VID, 2 * U), BF),
+        (*parts, w, gain, after),
+        2 * (27000 + (TR - 2) * 416 * 18) * 65536,
+        scratch=[
+            pltpu.VMEM((TR + 2, TC + 2, 2 * VID, C), BF),
+            pltpu.VMEM((TR + 2, TC + 1, 2 * VID, C), BF),
+        ],
+    )
 
 
 def ramp(pos, table_ref, amount, place):
@@ -462,11 +478,11 @@
     x, we, dl, dr, side_even, side_odd = edge(pos, tok, by_even, by_odd, cache, entry_weight, cm, wt, w, gain)
     side_even = swap(side_even, "cols", 0)
     side_odd = swap(side_odd, "cols", 1)
-    d, s = rest(x, we, cm, wt, dl, dr)
-    to_even, to_odd = join(pos, *strips(d, s, w, gain), side_even, side_odd)
+    rows = ends(x, we, cm, wt, dl, dr)
+    to_even, to_odd = join(pos, *strips(rows, w, gain), side_even, side_odd)
     by_odd = swap(to_odd, "rows", 1)
     by_even = swap(to_even, "rows", 0)
-    u = upper(d, s, w, gain, to_even)
+    u = upper((x, we, cm, wt, dl, dr, *rows), w, gain, to_even)
     out = lower(pos, row_ramp, col_ramp, u, side_even, side_odd, by_even, by_odd)
     return jnp.transpose(out, (0, 2, 1, 3))
 

time: 49 us -> 47.2 us (0.963)
  the two profiles are of different devices: /device:TPU:38 before, /device:TPU:59 now
where the time goes in v4:
time: 47.2 us; the launch traced here: 47 us
  Pallas kernels  26.3 us (56%)
  starting transfers between devices  14.3 us (30%)
  local copies, waits for them, and re-layouts  3.57 us (8%)
  waiting for transfers between devices  1.38 us (3%)
  other arithmetic  1.15 us (2%)
    pallas_call x7, Pallas kernels, call(): pl.pallas_call(body, in_specs=specs, out_specs=jax.tree.map(lambda _: VM,...  26.3 us
    ppermute x6, starting transfers between devices, swap(): return lax.ppermute(value, axis, pairs + [(j, i) for i, j in pairs])  14.3 us
    transpose x1, local copies, waits for them, and re-layouts, per_device(): jnp.transpose(cache_middle, (2, 3, 0, 1, 4)).reshape(TR * TC * VID, 2 * C)  3.3 us
    ppermute x6, waiting for transfers between devices, swap(): return lax.ppermute(value, axis, pairs + [(j, i) for i, j in pairs])  1.38 us
    select_n x1, other arithmetic, per_device(): by_odd = swap(jnp.where(even, first, last), 'rows', 1)  1.07 us
  transfers between devices with their start and end apart: 6, of which 2 were waited for; matrix products, arithmetic and copies ran while one was open for 7% of the time, Pallas kernels for 37%

profile of v4, /device:TPU:59, one launch (start us, length us, event | category | flops | bytes accessed | tf_op | source)
XLA Modules:
  0.0 47.0 jit_solution(3668312603084876853)
XLA Ops:
  0.0 1.1 %broadcast_select_fusion = (bf16[8,64,52]{2,1,0:T(8,128)(2,1)S(1)}, bf16[8,64,52]{2,1,0:T(8,128)(2,1)S(1)}) fusion(pred[]{:T(512)S(6)} %eq.5, bf16[8,64,208]{2,1,0:T(8,128)(2,1)} %bitcast.14), kind=kLoop, calls=%fused_computation | loop fusion | flops 53248 | bytes 212993 | tf_op jit(solution)/shard_map/jit(_where)/select_n | solution.py:469
  1.1 3.3 %collective-permute-start.1 = (bf16[8,64,52]{2,1,0:T(8,128)(2,1)S(1)}, bf16[8,64,52]{2,1,0:T(8,128)(2,1)S(1)}, u32[]{:S(2)}, u32[]{:S(2)}) collective-permute-start(bf16[8,64,52]{2,1,0:T(8,128)(2,1)S(1)} %get-tuple-element.33), channel_id=1, source_target_pairs={{4,8},{12,16},{20,24},{28,32},{36,40},{44,48},{52,56},{60,64},{68,... | collective-permute-start | bytes 159752 | tf_op jit(solution)/shard_map/ppermute | solution.py:22
  4.4 0.1 collective-permute-start
  4.5 0.1 pad_add_fusion.pos_ref
  4.6 0.0 copy-start
  4.6 3.3 %copy.10 = bf16[10,28,8,2,384]{4,2,3,1,0:T(8,128)(2,1)S(1)} copy(bf16[10,28,8,2,384]{4,3,1,0,2:T(2,128)(2,1)} %bitcast.23) | data formatting | bytes 6881280 | tf_op jit(solution)/shard_map/transpose | solution.py:472
  7.9 0.0 copy-done
  7.9 0.0 copy-start.1
  7.9 0.0 copy-start.4
  7.9 0.0 copy-start.5
  8.0 0.0 copy-start.6
  8.0 0.0 copy-start.7
  8.0 0.5 fold.1.w_ref.refs_10_
  8.4 1.0 %collective-permute-done.1.after_ref = bf16[8,64,52]{2,1,0:T(8,128)(2,1)S(1)} collective-permute-done((bf16[8,64,52]{2,1,0:T(8,128)(2,1)S(1)}, bf16[8,64,52]{2,1,0:T(8,128)(2,1)S(1)}, u32[]{:S(2)}, u32[]{:S(2)}) %collective-permute-start.1) | collective-permute-done | bytes 53280 | tf_op jit(solution)/shard_map/ppermute | solution.py:22
  9.5 0.0 collective-permute-done.before_ref
  9.5 0.0 copy-done.1
  9.5 0.0 copy-done.4
  9.5 0.1 copy-done.5
  9.6 0.1 copy-done.6
  9.7 0.0 copy-done.7
  9.7 4.5 %edge.1 = (bf16[2880,128]{1,0:T(8,128)(2,1)S(1)}, bf16[144,1152]{1,0:T(8,128)(2,1)S(1)}, bf16[12,3,16,384]{3,2,1,0:T(8,128)(2,1)S(1)}, bf16[12,3,16,384]{3,2,1,0...) custom-call(s32[2]{0:T(128)S(1)} %pad_add_fusion.pos_ref, ...), custom_call_target="tpu_custom_call" | custom-call | flops 5242880000 | bytes 65536 | tf_op jit(solution)/shard_map/edge/pallas_call | solution.py:40
  14.2 0.1 collective-permute-start.2
  14.3 4.9 %collective-permute-start.3 = (bf16[10,2,16,384]{3,2,1,0:T(8,128)(2,1)S(1)}, bf16[10,2,16,384]{3,2,1,0:T(8,128)(2,1)S(1)}, u32[]{:S(2)}, u32[]{:S(2)}) collective-permute-start(bf16[10,2,16,384]{3,2,1,0:T(8,128)(2,1)S(1)} %get-tuple-element.30), channel_id=1, source_target_pairs={{1,2},{2,1},{5,6},{6,5},{9,10},{10,9},{13,14},{14,13},{17,18},{18,... | collective-permute-start | bytes 737288 | tf_op jit(solution)/shard_map/ppermute | solution.py:22
  19.1 2.7 %ends.1 = (bf16[3,30,16,384]{3,2,1,0:T(8,128)(2,1)S(1)}, bf16[3,29,16,384]{3,2,1,0:T(8,128)(2,1)S(1)}, bf16[3,30,16,384]{3,2,1,0:T(8,128)(2,1)S(1)}, bf16[3,29,16,384]{3,2,1,0:T(8,128)(2,1)S(1)}) custom-call(bf16[2880,128]{1,0:T(8,128)(2,1)S(1)} %get-tuple-element.19.x_ref.refs_0_, bf16[144,1152]{1,0:T(8,128)(2,1)S(1)} %get-tuple-element.20.we_ref.refs_1_, ...), custom_call_target="tpu_custom_call" | custom-call | flops 2359296000 | bytes 65536 | tf_op jit(solution)/shard_map/ends/pallas_call | solution.py:40
  21.8 2.5 %strips.1 = (bf16[2,26,16,384]{3,2,1,0:T(8,128)(2,1)S(1)}, bf16[2,26,16,384]{3,2,1,0:T(8,128)(2,1)S(1)}) custom-call(bf16[3,30,16,384]{3,2,1,0:T(8,128)(2,1)S(1)} %get-tuple-element.23.td_ref.refs_6_, bf16[3,29,16,384]{3,2,1,0:T(8,128)(2,1)S(1)} %get-tuple-element.24.ts_ref.refs_7_, bf16[3,30,16,384]{3,2,1,0:T(8,128)(2,1)S(1)} %get-tuple-element.25.ld_ref.refs_8_, ...), custom_call_target="tpu_custom_call" | custom-call | flops 1962934272 | bytes 65536 | tf_op jit(solution)/shard_map/strips/pallas_call | solution.py:40
  24.3 0.0 collective-permute-done.2.se_ref
  24.4 0.3 collective-permute-done.3.so_ref
  24.7 0.7 %join.1 = (bf16[2,28,16,384]{3,2,1,0:T(8,128)(2,1)S(1)}, bf16[2,28,16,384]{3,2,1,0:T(8,128)(2,1)S(1)}) custom-call(s32[2]{0:T(128)S(1)} %pad_add_fusion.pos_ref, bf16[2,26,16,384]{3,2,1,0:T(8,128)(2,1)S(1)} %get-tuple-element.27.t_ref, bf16[2,26,16,384]{3,2,1,0:T(8,128)(2,1)S(1)} %get-tuple-element.28.l_ref, ...), custom_call_target="tpu_custom_call" | custom-call | flops 1048576 | bytes 65536 | tf_op jit(solution)/shard_map/join/pallas_call | solution.py:40
  25.4 5.7 %collective-permute-start.5 = (bf16[2,28,16,384]{3,2,1,0:T(8,128)(2,1)S(1)}, bf16[2,28,16,384]{3,2,1,0:T(8,128)(2,1)S(1)}, u32[]{:S(2)}, u32[]{:S(2)}) collective-permute-start(bf16[2,28,16,384]{3,2,1,0:T(8,128)(2,1)S(1)} %get-tuple-element.32), channel_id=1, source_target_pairs={{4,8},{12,16},{20,24},{28,32},{36,40},{44,48},{52,56},{60,64},{68,... | collective-permute-start | bytes 2064392 | tf_op jit(solution)/shard_map/ppermute | solution.py:22
  31.0 0.0 copy-start.2
  31.1 0.0 copy-start.3
  31.1 0.3 collective-permute-start.4
  31.3 11.8 %upper.1.u_ref = bf16[16,26,16,384]{3,2,1,0:T(8,128)(2,1)S(1)} custom-call(bf16[2880,128]{1,0:T(8,128)(2,1)S(1)} %get-tuple-element.19.x_ref.refs_0_, bf16[144,1152]{1,0:T(8,128)(2,1)S(1)} %get-tuple-element.20.we_ref.refs_1_, bf16[2240,768]{1,0:T(8,128)(2,1)S(1)} %bitcast.12, bf16[1152,768]{1,0:T(8,128)(2,1)S(1)} %bitcast.18, ...), custom_call_target="tpu_custom_call" | custom-call | flops 11390681088 | bytes 65536 | tf_op jit(solution)/shard_map/upper/pallas_call | solution.py:40
  43.1 0.0 collective-permute-done.5.odd_ref
  43.1 0.0 collective-permute-done.4.even_ref
  43.1 0.0 copy-done.2
  43.1 0.0 copy-done.3
  43.1 3.7 %lower.1 = bf16[8,52,16,384]{3,2,1,0:T(8,128)(2,1)} custom-call(s32[2]{0:T(128)S(1)} %pad_add_fusion.pos_ref, s32[32]{0:T(128)S(1)} %copy-done.2, s32[4]{0:T(128)S(1)} %copy-done.3, bf16[16,26,16,384]{3,2,1,0:T(8,128)(2,1)S(1)} %upper.1.u_ref, bf16[10,2,16,384]{3,2,1,0:T(8,128)(2,1)S(1)} %collective-permute-done.2.se_ref, ...), custom_call_target="tpu_custom_call" | custom-call | flops 1048576 | bytes 65536 | tf_op jit(solution)/shard_map/lower/pallas_call | solution.py:40
Async XLA Ops:
  1.1 8.4 %collective-permute-start.1 = (bf16[8,64,52]{2,1,0:T(8,128)(2,1)S(1)}, bf16[8,64,52]{2,1,0:T(8,128)(2,1)S(1)}, u32[]{:S(2)}, u32[]{:S(2)}) collective-permute-start(bf16[8,64,52]{2,1,0:T(8,128)(2,1)S(1)} %get-tuple-element.33), channel_id=1, source_target_pairs={{4,8},{12,16},{20,24},{28,32},{36,40},{44,48},{52,56},{60,64},{68,... | collective-permute-start | bytes 159752 | tf_op jit(solution)/shard_map/ppermute | solution.py:22
  4.4 5.1 %collective-permute-start = (bf16[8,64,52]{2,1,0:T(8,128)(2,1)S(1)}, bf16[8,64,52]{2,1,0:T(8,128)(2,1)S(1)}, u32[]{:S(2)}, u32[]{:S(2)}) collective-permute-start(bf16[8,64,52]{2,1,0:T(8,128)(2,1)S(1)} %get-tuple-element.34), channel_id=1, source_target_pairs={{0,4},{8,12},{16,20},{24,28},{32,36},{40,44},{48,52},{56,60},{64,6... | collective-permute-start | bytes 159752 | tf_op jit(solution)/shard_map/ppermute | solution.py:22
  4.6 3.3 %copy-start = (bf16[3,3,384,192]{2,3,1,0:T(8,128)(2,1)S(1)}, bf16[3,3,384,192]{2,3,1,0:T(8,128)(2,1)}, u32[]{:S(2)}) copy-start(bf16[3,3,384,192]{2,3,1,0:T(8,128)(2,1)} %param.14) | copy-start | bytes 3981316
  7.9 1.6 %copy-start.1 = (bf16[8,208,64]{1,2,0:T(8,128)(2,1)S(1)}, bf16[8,208,64]{1,2,0:T(8,128)(2,1)}, u32[]{:S(2)}) copy-start(bf16[8,208,64]{1,2,0:T(8,128)(2,1)} %param.9) | copy-start | bytes 638980
  7.9 1.6 %copy-start.4 = (bf16[3,384,768]{2,1,0:T(8,128)(2,1)S(1)}, bf16[3,384,768]{2,1,0:T(8,128)(2,1)}, u32[]{:S(2)}) copy-start(bf16[3,384,768]{2,1,0:T(8,128)(2,1)} %param.13) | copy-start | bytes 5308420
  7.9 1.7 %copy-start.5 = (bf16[8,2,10,28,16]{3,4,2,1,0:T(8,128)(2,1)S(1)}, bf16[8,2,10,28,16]{3,4,2,1,0:T(8,128)(2,1)}, u32[]{:S(2)}) copy-start(bf16[8,2,10,28,16]{3,4,2,1,0:T(8,128)(2,1)} %param.10) | copy-start | bytes 430084
  8.0 1.8 %copy-start.6 = (bf16[3,3,3,16,384]{4,3,2,1,0:T(8,128)(2,1)S(1)}, bf16[3,3,3,16,384]{4,3,2,1,0:T(8,128)(2,1)}, u32[]{:S(2)}) copy-start(bf16[3,3,3,16,384]{4,3,2,1,0:T(8,128)(2,1)} %ew_ref.1) | copy-start | bytes 995332
  8.0 1.7 %copy-start.7 = (f32[192]{0:T(256)S(1)}, f32[192]{0:T(256)}, u32[]{:S(2)}) copy-start(f32[192]{0:T(256)} %param.15) | copy-start | bytes 2308
  14.2 10.2 %collective-permute-start.2 = (bf16[10,2,16,384]{3,2,1,0:T(8,128)(2,1)S(1)}, bf16[10,2,16,384]{3,2,1,0:T(8,128)(2,1)S(1)}, u32[]{:S(2)}, u32[]{:S(2)}) collective-permute-start(bf16[10,2,16,384]{3,2,1,0:T(8,128)(2,1)S(1)} %get-tuple-element.29), channel_id=1, source_target_pairs={{0,1},{2,3},{1,0},{3,2},{4,5},{6,7},{5,4},{7,6},{8,9},{10,11},{9,8... | collective-permute-start | bytes 737288 | tf_op jit(solution)/shard_map/ppermute | solution.py:22
  14.3 10.4 %collective-permute-start.3 = (bf16[10,2,16,384]{3,2,1,0:T(8,128)(2,1)S(1)}, bf16[10,2,16,384]{3,2,1,0:T(8,128)(2,1)S(1)}, u32[]{:S(2)}, u32[]{:S(2)}) collective-permute-start(bf16[10,2,16,384]{3,2,1,0:T(8,128)(2,1)S(1)} %get-tuple-element.30), channel_id=1, source_target_pairs={{1,2},{2,1},{5,6},{6,5},{9,10},{10,9},{13,14},{14,13},{17,18},{18,... | collective-permute-start | bytes 737288 | tf_op jit(solution)/shard_map/ppermute | solution.py:22
  25.4 17.7 %collective-permute-start.5 = (bf16[2,28,16,384]{3,2,1,0:T(8,128)(2,1)S(1)}, bf16[2,28,16,384]{3,2,1,0:T(8,128)(2,1)S(1)}, u32[]{:S(2)}, u32[]{:S(2)}) collective-permute-start(bf16[2,28,16,384]{3,2,1,0:T(8,128)(2,1)S(1)} %get-tuple-element.32), channel_id=1, source_target_pairs={{4,8},{12,16},{20,24},{28,32},{36,40},{44,48},{52,56},{60,64},{68,... | collective-permute-start | bytes 2064392 | tf_op jit(solution)/shard_map/ppermute | solution.py:22
  31.0 12.1 %copy-start.2 = (s32[32]{0:T(128)S(1)}, s32[32]{0:T(128)}, u32[]{:S(2)}) copy-start(s32[32]{0:T(128)} %rr_ref.1) | copy-start | bytes 388
  31.1 12.1 %copy-start.3 = (s32[4]{0:T(128)S(1)}, s32[4]{0:T(128)}, u32[]{:S(2)}) copy-start(s32[4]{0:T(128)} %cr_ref.1) | copy-start | bytes 52
  31.1 12.0 %collective-permute-start.4 = (bf16[2,28,16,384]{3,2,1,0:T(8,128)(2,1)S(1)}, bf16[2,28,16,384]{3,2,1,0:T(8,128)(2,1)S(1)}, u32[]{:S(2)}, u32[]{:S(2)}) collective-permute-start(bf16[2,28,16,384]{3,2,1,0:T(8,128)(2,1)S(1)} %get-tuple-element.31.refs_12_), channel_id=1, source_target_pairs={{0,4},{8,12},{16,20},{24,28},{32,36},{40,44},{48,52},{56,60},{64,6... | collective-permute-start | bytes 2064392 | tf_op jit(solution)/shard_map/ppermute | solution.py:22

commit v5 on v4

--- a/solution.py
+++ b/solution.py
@@ -123,7 +123,7 @@
     ew_ref,
     cm_ref,
     wt_ref,
-    w_ref,
+    ut_ref,
     gain_ref,
     x_ref,
     we_ref,
@@ -131,12 +131,14 @@
     dr_ref,
     even_ref,
     odd_ref,
+    w_ref,
     t_ref,
     lat_ref,
     old_ref,
     sl_ref,
     sr_ref,
 ):
+    fold_body(ut_ref, w_ref)
     dl_ref[...] = jnp.zeros(dl_ref.shape, BF)
     dr_ref[...] = jnp.zeros(dr_ref.shape, BF)
     for f in range(3):
@@ -157,15 +159,16 @@
         odd_ref[:, a] = either(pos_ref[1], v[:TR].astype(F32), v[TR:].astype(F32), 2 * VID).astype(BF)
 
 
-def edge(pos, tok, before, after, cache, ew, cm, wt, w, gain):
+def edge(pos, tok, before, after, cache, ew, cm, wt, ut, gain):
     part = pltpu.VMEM((TR + 2, 3, 2 * VID, C), BF)
     side = jax.ShapeDtypeStruct((TR, 2, 2 * VID, 2 * U), BF)
     outs = (pltpu.VMEM((12 * WIDE, 128), BF), pltpu.VMEM((144, 3 * C), BF), part, part, side, side)
+    outs += (pltpu.VMEM((2, 3, 256, 2 * C), BF),)
     return call(
         edge_body,
         "edge",
         outs,
-        (pos, tok, before, after, cache, ew, cm, wt, w, gain),
+        (pos, tok, before, after, cache, ew, cm, wt, ut, gain),
         2 * 40000 * 65536,
         scratch=[
             pltpu.VMEM((2, 6 * PITCH + 8, 128), F32),
@@ -189,12 +192,6 @@
         d_ref[at : at + 2, 3 : n + 3] = d.reshape(2, n, 2 * VID, C)
         for i in range(3):
             s_ref[i : i + 1] = steps_right(d_ref[i : i + 1])
-
-
-def ends(x, we, cm, wt, dl, dr):
-    part = pltpu.VMEM((3, TC + 2, 2 * VID, C), BF)
-    step = pltpu.VMEM((3, TC + 1, 2 * VID, C), BF)
-    return call(ends_body, "ends", (part, step, part, step), (x, we, cm, wt, dl, dr), 2 * 18000 * 65536)
 
 
 def rest_body(x_ref, we_ref, cm_ref, wt_ref, dl_ref, dr_ref, td_ref, ts_ref, ld_ref, ls_ref, d_ref, s_ref):
@@ -221,10 +218,6 @@
                 w = w.astype(BF)
                 w_ref[a, k, 0:U, kr * C : (kr + 1) * C] = w
                 w_ref[a, k, U:256, kr * C : (kr + 1) * C] = w[0:64]
-
-
-def fold(ut):
-    return call(fold_body, "fold", pltpu.VMEM((2, 3, 256, 2 * C), BF), (ut,), 1 << 24)
 
 
 def steps_right(value):
@@ -289,9 +282,18 @@
             ref[a] = both(w_ref, gain, ((d_ref, s_ref, 0, 1, 1, n),), a)
 
 
-def strips(rows, w, gain):
+def margins_body(*refs):
+    (w_ref, gain_ref), rows, tops = refs[6:8], refs[8:12], refs[12:]
+    ends_body(*refs[:6], *rows)
+    strips_body(*rows, w_ref, gain_ref, *tops)
+
+
+def margins(x, we, cm, wt, dl, dr, w, gain):
+    part = pltpu.VMEM((3, TC + 2, 2 * VID, C), BF)
+    step = pltpu.VMEM((3, TC + 1, 2 * VID, C), BF)
     strip = pltpu.VMEM((2, TC - 2, 2 * VID, 2 * U), BF)
-    return call(strips_body, "strips", (strip, strip), (*rows, w, gain), 2 * 832 * 18 * 65536)
+    args = (x, we, cm, wt, dl, dr, w, gain)
+    return call(margins_body, "margins", (part, step, part, step, strip, strip), args, 2 * 33000 * 65536)
 
 
 def join_body(pos_ref, t_ref, l_ref, se_ref, so_ref, even_ref, odd_ref):
@@ -474,12 +476,11 @@
     ut = jnp.transpose(up_weight, (0, 1, 3, 2))
     gain = norm_gain.reshape(1, U)
     pos = jnp.stack([row_pos, col_pos]).astype(jnp.int32)
-    w = fold(ut)
-    x, we, dl, dr, side_even, side_odd = edge(pos, tok, by_even, by_odd, cache, entry_weight, cm, wt, w, gain)
+    x, we, dl, dr, side_even, side_odd, w = edge(pos, tok, by_even, by_odd, cache, entry_weight, cm, wt, ut, gain)
     side_even = swap(side_even, "cols", 0)
     side_odd = swap(side_odd, "cols", 1)
-    rows = ends(x, we, cm, wt, dl, dr)
-    to_even, to_odd = join(pos, *strips(rows, w, gain), side_even, side_odd)
+    *rows, top, low = margins(x, we, cm, wt, dl, dr, w, gain)
+    to_even, to_odd = join(pos, top, low, side_even, side_odd)
     by_odd = swap(to_odd, "rows", 1)
     by_even = swap(to_even, "rows", 0)
     u = upper((x, we, cm, wt, dl, dr, *rows), w, gain, to_even)

time: 47.2 us -> 47.5 us (level)
  the two profiles are of different devices: /device:TPU:59 before, /device:TPU:67 now
where the time goes in v5:
time: 47.5 us; the launch traced here: 47.3 us
  Pallas kernels  26.4 us (56%)
  starting transfers between devices  14.3 us (30%)
  local copies, waits for them, and re-layouts  3.38 us (7%)
  waiting for transfers between devices  1.79 us (4%)
  other arithmetic  1.15 us (2%)
    pallas_call x5, Pallas kernels, call(): pl.pallas_call(body, in_specs=specs, out_specs=jax.tree.map(lambda _: VM,...  26.4 us
    ppermute x6, starting transfers between devices, swap(): return lax.ppermute(value, axis, pairs + [(j, i) for i, j in pairs])  14.3 us
    transpose x1, local copies, waits for them, and re-layouts, per_device(): jnp.transpose(cache_middle, (2, 3, 0, 1, 4)).reshape(TR * TC * VID, 2 * C)  3.35 us
    ppermute x6, waiting for transfers between devices, swap(): return lax.ppermute(value, axis, pairs + [(j, i) for i, j in pairs])  1.79 us
    select_n x1, other arithmetic, per_device(): by_odd = swap(jnp.where(even, first, last), 'rows', 1)  1.07 us
  transfers between devices with their start and end apart: 6, of which 1 were waited for; matrix products, arithmetic and copies ran while one was open for 7% of the time, Pallas kernels for 37%

profile of v5, /device:TPU:67, one launch (start us, length us, event | category | flops | bytes accessed | tf_op | source)
XLA Modules:
  0.0 47.3 jit_solution(12414881584246351919)
XLA Ops:
  0.0 1.1 %broadcast_select_fusion = (bf16[8,64,52]{2,1,0:T(8,128)(2,1)S(1)}, bf16[8,64,52]{2,1,0:T(8,128)(2,1)S(1)}) fusion(pred[]{:T(512)S(6)} %eq.5, bf16[8,64,208]{2,1,0:T(8,128)(2,1)} %bitcast.13), kind=kLoop, calls=%fused_computation | loop fusion | flops 53248 | bytes 212993 | tf_op jit(solution)/shard_map/jit(_where)/select_n | solution.py:471
  1.1 3.8 %collective-permute-start.1 = (bf16[8,64,52]{2,1,0:T(8,128)(2,1)S(1)}, bf16[8,64,52]{2,1,0:T(8,128)(2,1)S(1)}, u32[]{:S(2)}, u32[]{:S(2)}) collective-permute-start(bf16[8,64,52]{2,1,0:T(8,128)(2,1)S(1)} %get-tuple-element.35), channel_id=1, source_target_pairs={{4,8},{12,16},{20,24},{28,32},{36,40},{44,48},{52,56},{60,64},{68,... | collective-permute-start | bytes 159752 | tf_op jit(solution)/shard_map/ppermute | solution.py:22
  4.9 1.3 %collective-permute-start = (bf16[8,64,52]{2,1,0:T(8,128)(2,1)S(1)}, bf16[8,64,52]{2,1,0:T(8,128)(2,1)S(1)}, u32[]{:S(2)}, u32[]{:S(2)}) collective-permute-start(bf16[8,64,52]{2,1,0:T(8,128)(2,1)S(1)} %get-tuple-element.36), channel_id=1, source_target_pairs={{0,4},{8,12},{16,20},{24,28},{32,36},{40,44},{48,52},{56,60},{64,6... | collective-permute-start | bytes 159752 | tf_op jit(solution)/shard_map/ppermute | solution.py:22
  6.2 0.1 pad_add_fusion.pos_ref
  6.3 0.0 copy-start
  6.3 0.0 copy-start.3
  6.3 0.0 copy-start.4
  6.3 0.0 copy-start.5
  6.3 0.0 copy-start.6
  6.3 0.0 copy-start.7
  6.3 3.3 %copy.10 = bf16[10,28,8,2,384]{4,2,3,1,0:T(8,128)(2,1)S(1)} copy(bf16[10,28,8,2,384]{4,3,1,0,2:T(2,128)(2,1)} %bitcast.23) | data formatting | bytes 6881280 | tf_op jit(solution)/shard_map/transpose | solution.py:474
  9.6 0.0 collective-permute-done.1.after_ref
  9.6 0.0 collective-permute-done.before_ref
  9.7 0.0 copy-done
  9.7 0.0 copy-done.3
  9.7 0.0 copy-done.4
  9.7 0.0 copy-done.5
  9.7 0.0 copy-done.6
  9.7 0.0 copy-done.7
  9.7 4.6 %edge.1 = (bf16[2880,128]{1,0:T(8,128)(2,1)S(1)}, bf16[144,1152]{1,0:T(8,128)(2,1)S(1)}, bf16[12,3,16,384]{3,2,1,0:T(8,128)(2,1)S(1)}, bf16[12,3,16,384]{3,2,1,0...) custom-call(s32[2]{0:T(128)S(1)} %pad_add_fusion.pos_ref, ...), custom_call_target="tpu_custom_call" | custom-call | flops 5242880000 | bytes 65536 | tf_op jit(solution)/shard_map/edge/pallas_call | solution.py:40
  14.4 1.4 %collective-permute-start.2 = (bf16[10,2,16,384]{3,2,1,0:T(8,128)(2,1)S(1)}, bf16[10,2,16,384]{3,2,1,0:T(8,128)(2,1)S(1)}, u32[]{:S(2)}, u32[]{:S(2)}) collective-permute-start(bf16[10,2,16,384]{3,2,1,0:T(8,128)(2,1)S(1)} %get-tuple-element.31), channel_id=1, source_target_pairs={{0,1},{2,3},{1,0},{3,2},{4,5},{6,7},{5,4},{7,6},{8,9},{10,11},{9,8... | collective-permute-start | bytes 737288 | tf_op jit(solution)/shard_map/ppermute | solution.py:22
  15.8 1.9 %collective-permute-start.3 = (bf16[10,2,16,384]{3,2,1,0:T(8,128)(2,1)S(1)}, bf16[10,2,16,384]{3,2,1,0:T(8,128)(2,1)S(1)}, u32[]{:S(2)}, u32[]{:S(2)}) collective-permute-start(bf16[10,2,16,384]{3,2,1,0:T(8,128)(2,1)S(1)} %get-tuple-element.32), channel_id=1, source_target_pairs={{1,2},{2,1},{5,6},{6,5},{9,10},{10,9},{13,14},{14,13},{17,18},{18,... | collective-permute-start | bytes 737288 | tf_op jit(solution)/shard_map/ppermute | solution.py:22
  17.7 4.9 %margins.1 = (bf16[3,30,16,384]{3,2,1,0:T(8,128)(2,1)S(1)}, bf16[3,29,16,384]{3,2,1,0:T(8,128)(2,1)S(1)}, bf16[3,30,16,384]{3,2,1,0:T(8,128)(2,1)S(1)}, bf16[3,2...) custom-call(bf16[2880,128]{1,0:T(8,128)(2,1)S(1)} %get-tuple-element.20.refs, ...), custom_call_target="tpu_custom_call" | custom-call | flops 4325376000 | bytes 65536 | tf_op jit(solution)/shard_map/margins/pallas_call | solution.py:40
  22.6 0.0 collective-permute-done.2.se_ref
  22.6 1.8 %collective-permute-done.3.so_ref = bf16[10,2,16,384]{3,2,1,0:T(8,128)(2,1)S(1)} collective-permute-done((bf16[10,2,16,384]{3,2,1,0:T(8,128)(2,1)S(1)}, bf16[10,2,16,384]{3,2,1,0:T(8,128)(2,1)S(1)}, u32[]{:S(2)}, u32[]{:S(2)}) %collective-permute-start.3) | collective-permute-done | bytes 245792 | tf_op jit(solution)/shard_map/ppermute | solution.py:22
  24.4 0.7 %join.1 = (bf16[2,28,16,384]{3,2,1,0:T(8,128)(2,1)S(1)}, bf16[2,28,16,384]{3,2,1,0:T(8,128)(2,1)S(1)}) custom-call(s32[2]{0:T(128)S(1)} %pad_add_fusion.pos_ref, bf16[2,26,16,384]{3,2,1,0:T(8,128)(2,1)S(1)} %get-tuple-element.29.t_ref, bf16[2,26,16,384]{3,2,1,0:T(8,128)(2,1)S(1)} %get-tuple-element.30.l_ref, ...), custom_call_target="tpu_custom_call" | custom-call | flops 1048576 | bytes 65536 | tf_op jit(solution)/shard_map/join/pallas_call | solution.py:40
  25.1 3.5 %collective-permute-start.5 = (bf16[2,28,16,384]{3,2,1,0:T(8,128)(2,1)S(1)}, bf16[2,28,16,384]{3,2,1,0:T(8,128)(2,1)S(1)}, u32[]{:S(2)}, u32[]{:S(2)}) collective-permute-start(bf16[2,28,16,384]{3,2,1,0:T(8,128)(2,1)S(1)} %get-tuple-element.34), channel_id=1, source_target_pairs={{4,8},{12,16},{20,24},{28,32},{36,40},{44,48},{52,56},{60,64},{68,... | collective-permute-start | bytes 2064392 | tf_op jit(solution)/shard_map/ppermute | solution.py:22
  28.6 2.4 %collective-permute-start.4 = (bf16[2,28,16,384]{3,2,1,0:T(8,128)(2,1)S(1)}, bf16[2,28,16,384]{3,2,1,0:T(8,128)(2,1)S(1)}, u32[]{:S(2)}, u32[]{:S(2)}) collective-permute-start(bf16[2,28,16,384]{3,2,1,0:T(8,128)(2,1)S(1)} %get-tuple-element.33.refs_12_), channel_id=1, source_target_pairs={{0,4},{8,12},{16,20},{24,28},{32,36},{40,44},{48,52},{56,60},{64,6... | collective-permute-start | bytes 2064392 | tf_op jit(solution)/shard_map/ppermute | solution.py:22
  30.9 0.0 copy-start.1
  31.0 0.0 copy-start.2
  31.0 12.4 %upper.1.u_ref = bf16[16,26,16,384]{3,2,1,0:T(8,128)(2,1)S(1)} custom-call(bf16[2880,128]{1,0:T(8,128)(2,1)S(1)} %get-tuple-element.20.refs_0_, bf16[144,1152]{1,0:T(8,128)(2,1)S(1)} %get-tuple-element.21.refs_1_, bf16[2240,768]{1,0:T(8,128)(2,1)S(1)} %bitcast.12, bf16[1152,768]{1,0:T(8,128)(2,1)S(1)} %bitcast.17, ...), custom_call_target="tpu_custom_call" | custom-call | flops 11390681088 | bytes 65536 | tf_op jit(solution)/shard_map/upper/pallas_call | solution.py:40
  43.4 0.0 collective-permute-done.5.odd_ref
  43.4 0.0 collective-permute-done.4.even_ref
  43.4 0.0 copy-done.1
  43.4 0.0 copy-done.2
  43.4 3.7 %lower.1 = bf16[8,52,16,384]{3,2,1,0:T(8,128)(2,1)} custom-call(s32[2]{0:T(128)S(1)} %pad_add_fusion.pos_ref, s32[32]{0:T(128)S(1)} %copy-done.1, s32[4]{0:T(128)S(1)} %copy-done.2, bf16[16,26,16,384]{3,2,1,0:T(8,128)(2,1)S(1)} %upper.1.u_ref, bf16[10,2,16,384]{3,2,1,0:T(8,128)(2,1)S(1)} %collective-permute-done.2.se_ref, ...), custom_call_target="tpu_custom_call" | custom-call | flops 1048576 | bytes 65536 | tf_op jit(solution)/shard_map/lower/pallas_call | solution.py:40
Async XLA Ops:
  1.1 8.6 %collective-permute-start.1 = (bf16[8,64,52]{2,1,0:T(8,128)(2,1)S(1)}, bf16[8,64,52]{2,1,0:T(8,128)(2,1)S(1)}, u32[]{:S(2)}, u32[]{:S(2)}) collective-permute-start(bf16[8,64,52]{2,1,0:T(8,128)(2,1)S(1)} %get-tuple-element.35), channel_id=1, source_target_pairs={{4,8},{12,16},{20,24},{28,32},{36,40},{44,48},{52,56},{60,64},{68,... | collective-permute-start | bytes 159752 | tf_op jit(solution)/shard_map/ppermute | solution.py:22
  4.9 4.8 %collective-permute-start = (bf16[8,64,52]{2,1,0:T(8,128)(2,1)S(1)}, bf16[8,64,52]{2,1,0:T(8,128)(2,1)S(1)}, u32[]{:S(2)}, u32[]{:S(2)}) collective-permute-start(bf16[8,64,52]{2,1,0:T(8,128)(2,1)S(1)} %get-tuple-element.36), channel_id=1, source_target_pairs={{0,4},{8,12},{16,20},{24,28},{32,36},{40,44},{48,52},{56,60},{64,6... | collective-permute-start | bytes 159752 | tf_op jit(solution)/shard_map/ppermute | solution.py:22
  6.3 3.4 %copy-start = (bf16[8,208,64]{1,2,0:T(8,128)(2,1)S(1)}, bf16[8,208,64]{1,2,0:T(8,128)(2,1)}, u32[]{:S(2)}) copy-start(bf16[8,208,64]{1,2,0:T(8,128)(2,1)} %param.9) | copy-start | bytes 638980
  6.3 3.4 %copy-start.3 = (bf16[3,384,768]{2,1,0:T(8,128)(2,1)S(1)}, bf16[3,384,768]{2,1,0:T(8,128)(2,1)}, u32[]{:S(2)}) copy-start(bf16[3,384,768]{2,1,0:T(8,128)(2,1)} %param.13) | copy-start | bytes 5308420
  6.3 3.4 %copy-start.4 = (bf16[3,3,384,192]{2,3,1,0:T(8,128)(2,1)S(1)}, bf16[3,3,384,192]{2,3,1,0:T(8,128)(2,1)}, u32[]{:S(2)}) copy-start(bf16[3,3,384,192]{2,3,1,0:T(8,128)(2,1)} %param.14) | copy-start | bytes 3981316
  6.3 3.4 %copy-start.5 = (bf16[8,2,10,28,16]{3,4,2,1,0:T(8,128)(2,1)S(1)}, bf16[8,2,10,28,16]{3,4,2,1,0:T(8,128)(2,1)}, u32[]{:S(2)}) copy-start(bf16[8,2,10,28,16]{3,4,2,1,0:T(8,128)(2,1)} %param.10) | copy-start | bytes 430084
  6.3 3.4 %copy-start.6 = (bf16[3,3,3,16,384]{4,3,2,1,0:T(8,128)(2,1)S(1)}, bf16[3,3,3,16,384]{4,3,2,1,0:T(8,128)(2,1)}, u32[]{:S(2)}) copy-start(bf16[3,3,3,16,384]{4,3,2,1,0:T(8,128)(2,1)} %ew_ref.1) | copy-start | bytes 995332
  6.3 3.4 %copy-start.7 = (f32[192]{0:T(256)S(1)}, f32[192]{0:T(256)}, u32[]{:S(2)}) copy-start(f32[192]{0:T(256)} %param.15) | copy-start | bytes 2308
  14.4 8.2 %collective-permute-start.2 = (bf16[10,2,16,384]{3,2,1,0:T(8,128)(2,1)S(1)}, bf16[10,2,16,384]{3,2,1,0:T(8,128)(2,1)S(1)}, u32[]{:S(2)}, u32[]{:S(2)}) collective-permute-start(bf16[10,2,16,384]{3,2,1,0:T(8,128)(2,1)S(1)} %get-tuple-element.31), channel_id=1, source_target_pairs={{0,1},{2,3},{1,0},{3,2},{4,5},{6,7},{5,4},{7,6},{8,9},{10,11},{9,8... | collective-permute-start | bytes 737288 | tf_op jit(solution)/shard_map/ppermute | solution.py:22
  15.8 8.6 %collective-permute-start.3 = (bf16[10,2,16,384]{3,2,1,0:T(8,128)(2,1)S(1)}, bf16[10,2,16,384]{3,2,1,0:T(8,128)(2,1)S(1)}, u32[]{:S(2)}, u32[]{:S(2)}) collective-permute-start(bf16[10,2,16,384]{3,2,1,0:T(8,128)(2,1)S(1)} %get-tuple-element.32), channel_id=1, source_target_pairs={{1,2},{2,1},{5,6},{6,5},{9,10},{10,9},{13,14},{14,13},{17,18},{18,... | collective-permute-start | bytes 737288 | tf_op jit(solution)/shard_map/ppermute | solution.py:22
  25.1 18.3 %collective-permute-start.5 = (bf16[2,28,16,384]{3,2,1,0:T(8,128)(2,1)S(1)}, bf16[2,28,16,384]{3,2,1,0:T(8,128)(2,1)S(1)}, u32[]{:S(2)}, u32[]{:S(2)}) collective-permute-start(bf16[2,28,16,384]{3,2,1,0:T(8,128)(2,1)S(1)} %get-tuple-element.34), channel_id=1, source_target_pairs={{4,8},{12,16},{20,24},{28,32},{36,40},{44,48},{52,56},{60,64},{68,... | collective-permute-start | bytes 2064392 | tf_op jit(solution)/shard_map/ppermute | solution.py:22
  28.6 14.8 %collective-permute-start.4 = (bf16[2,28,16,384]{3,2,1,0:T(8,128)(2,1)S(1)}, bf16[2,28,16,384]{3,2,1,0:T(8,128)(2,1)S(1)}, u32[]{:S(2)}, u32[]{:S(2)}) collective-permute-start(bf16[2,28,16,384]{3,2,1,0:T(8,128)(2,1)S(1)} %get-tuple-element.33.refs_12_), channel_id=1, source_target_pairs={{0,4},{8,12},{16,20},{24,28},{32,36},{40,44},{48,52},{56,60},{64,6... | collective-permute-start | bytes 2064392 | tf_op jit(solution)/shard_map/ppermute | solution.py:22
  30.9 12.4 %copy-start.1 = (s32[32]{0:T(128)S(1)}, s32[32]{0:T(128)}, u32[]{:S(2)}) copy-start(s32[32]{0:T(128)} %rr_ref.1) | copy-start | bytes 388
  31.0 12.5 %copy-start.2 = (s32[4]{0:T(128)S(1)}, s32[4]{0:T(128)}, u32[]{:S(2)}) copy-start(s32[4]{0:T(128)} %cr_ref.1) | copy-start | bytes 52
